TPU v7x, 32 devices: a whole 2x2x4 slice. The times are simulated.
32 devices in a mesh: row: 4 (over z), dp: 4 (over y, x), mp: 2 (over core).
Axes of the slice: x: 2, y: 2, z: 4, core: 2. Of those that a mesh axis runs over, the one named last changes fastest.
Arguments:
- tokens: bfloat16 [16384, 640], P(('row', 'dp')), may hold values from -6 to 6
- encoder: bfloat16 [4, 16384, 640], P('row', 'dp'), may hold values from -6 to 6
- layer_pick: int32 [4, 4], replicated, may hold values from 0 to 1, as said below
- piece_heads: int32 [4], replicated, may hold values from 2 to 8, as said below
- piece_ffn: int32 [4], replicated, may hold values from 1024 to 3072, as said below
- tgt_len: int32 [64], P(('row', 'dp')), may hold values from 128 to 256, as said below
- src_len: int32 [64], P(('row', 'dp')), may hold values from 128 to 256, as said below
- norm_gain: float32 [3, 640], replicated, may hold values from 0.1 to 1.9
- norm_shift: float32 [3, 640], replicated, may hold values from -4 to 4
- out_bias: float32 [3, 640], replicated, may hold values from -4 to 4
- w_self: bfloat16 [3, 640, 640], P(None, None, 'mp'), may hold values from -0.3125 to 0.3125
- o_self: bfloat16 [640, 640], P('mp'), may hold values from -0.625 to 0.625
- b_self: float32 [2, 640], P(None, 'mp'), may hold values from -6 to 6
- w_cross: bfloat16 [3, 640, 640], P(None, None, 'mp'), may hold values from -0.3125 to 0.3125
- o_cross: bfloat16 [640, 640], P('mp'), may hold values from -0.625 to 0.625
- b_cross: float32 [2, 640], P(None, 'mp'), may hold values from -6 to 6
- w_up: bfloat16 [640, 3072], P(None, 'mp'), may hold values from -0.25 to 0.25
- b_up: float32 [3072], P('mp'), may hold values from -6 to 6
- w_down: bfloat16 [3072, 640], P('mp'), may hold values from -0.15625 to 0.15625
- cotangent: bfloat16 [16384, 640], P(('row', 'dp')), may hold values from -6 to 6
Outputs:
- block_out: float32 [16384, 640], P(('row', 'dp'))
- grad_tokens: float32 [16384, 640], P(('row', 'dp'))
- grad_encoder: float32 [4, 16384, 640], P('row', 'dp')
- grad_norm_gain: float32 [3, 640], P(None, ('row', 'dp'))
- grad_norm_shift: float32 [3, 640], P(None, ('row', 'dp'))
- grad_out_bias: float32 [3, 640], P(None, ('row', 'dp'))
- grad_w_self: float32 [3, 640, 640], P(None, ('row', 'dp'), 'mp')
- grad_o_self: float32 [640, 640], P('mp', ('row', 'dp'))
- grad_b_self: float32 [2, 640], P(None, 'mp')
- grad_w_cross: float32 [3, 640, 640], P(None, ('row', 'dp'), 'mp')
- grad_o_cross: float32 [640, 640], P('mp', ('row', 'dp'))
- grad_b_cross: float32 [2, 640], P(None, 'mp')
- grad_w_up: float32 [640, 3072], P(('row', 'dp'), 'mp')
- grad_b_up: float32 [3072], P('mp')
- grad_w_down: float32 [3072, 640], P('mp', ('row', 'dp'))
Inputs may be any that keep to these rules, and one draw needn't show every extreme that they name: `layer_pick`: each piece chooses 1 to 3 of the 4 layers (1 marks a chosen one); some piece chooses 3 and another 1. `piece_heads`: a piece uses heads 0 to this count - 1 in both attentions; some piece uses all 8. `piece_ffn`: a multiple of 1024; a piece uses units 0 to this - 1; some piece uses all 3072. `tgt_len`: among each aligned block of 4 sentences one has 256. `src_len`: among each aligned block of 4 sentences one has 256.
All inputs are finite; a program needn't handle non-finite values.
Results may differ from a plain program's by a relative error of at most 0.028.
The roundings to bfloat16 on the way count: a program that leaves them out, or rounds other values in their place, can miss the bound.
Values may be sent and summed in bfloat16 or wider, within the bound.
A program may use at most 192 MiB of HBM per device.

v0:
```python
import jax
import jax.numpy as jnp
from jax import lax
from jax.sharding import PartitionSpec as P

HD = 80


EPSILON = 1e-05
MASKED = -1e30


def layer_norm(stream, gain, shift):
    centre = stream - jnp.mean(stream, axis=-1, keepdims=True)
    spread = jnp.mean(centre * centre, axis=-1, keepdims=True)
    return centre * lax.rsqrt(spread + EPSILON) * gain + shift


def norm_back(stream, gain, shift, upstream):
    normed, pullback = jax.vjp(layer_norm, stream, gain, shift)
    return pullback(upstream)


def masked_scores(query_low, key_low, key_mask):
    raw_scores = jnp.einsum(
        "gqhd,gkhd->ghqk", query_low, key_low, preferred_element_type=jnp.float32
    )
    return jnp.where(key_mask[:, None], raw_scores * HD ** (-0.5), MASKED)


def attend_forward(query_low, key_low, value_low, key_mask):
    scores = masked_scores(query_low, key_low, key_mask)
    row_max = jnp.max(scores, axis=-1, keepdims=True)
    exp_scores = jnp.exp(scores - row_max)
    row_total = jnp.sum(exp_scores, axis=-1, keepdims=True)
    soft_probs = (exp_scores / row_total).astype(jnp.bfloat16)
    mixed_heads = jnp.einsum(
        "ghqk,gkhd->gqhd", soft_probs, value_low, preferred_element_type=jnp.float32
    )
    return (mixed_heads, row_max + jnp.log(row_total))


def attend_backward(query_low, key_low, value_low, key_mask, log_total, grad_heads):
    scores = masked_scores(query_low, key_low, key_mask)
    soft_probs = jnp.exp(scores - log_total)
    grad_value = jnp.einsum(
        "ghqk,gqhd->gkhd",
        soft_probs.astype(jnp.bfloat16),
        grad_heads,
        preferred_element_type=jnp.float32,
    )
    grad_prob = jnp.einsum(
        "gqhd,gkhd->ghqk", grad_heads, value_low, preferred_element_type=jnp.float32
    )
    row_delta = jnp.sum(soft_probs * grad_prob, axis=-1, keepdims=True)
    grad_score = (soft_probs * (grad_prob - row_delta) * HD ** (-0.5)).astype(jnp.bfloat16)
    grad_query = jnp.einsum(
        "ghqk,gkhd->gqhd", grad_score, key_low, preferred_element_type=jnp.float32
    )
    grad_key = jnp.einsum(
        "ghqk,gqhd->gkhd", grad_score, query_low, preferred_element_type=jnp.float32
    )
    return (grad_query, grad_key, grad_value)


def column_sum(values):
    return jnp.sum(values.astype(jnp.float32), axis=0)


def per_device(
    tokens,
    encoder,
    layer_pick,
    piece_heads,
    piece_ffn,
    tgt_len,
    src_len,
    norm_gain,
    norm_shift,
    out_bias,
    w_self,
    o_self,
    b_self,
    w_cross,
    o_cross,
    b_cross,
    w_up,
    b_up,
    w_down,
    cotangent,
):
    row_index = lax.axis_index("row")
    model_index = lax.axis_index("mp")
    row_count = lax.axis_size("row")
    seq_count = tgt_len.shape[0]
    tokens_count = tokens.shape[0]
    tgt_slots = tokens_count // seq_count
    src_slots = encoder.shape[1] // (row_count * seq_count)
    model_width = tokens.shape[1]
    local_heads = w_self.shape[2] // HD
    local_units = w_up.shape[1]
    pieces = layer_pick.shape[0]
    chosen = layer_pick.astype(jnp.float32)
    layer_weight = chosen / jnp.sum(chosen, axis=1, keepdims=True)
    own_piece = (jnp.arange(pieces) == row_index).astype(jnp.float32)
    own_weight = jnp.sum(own_piece[:, None] * layer_weight, axis=0)
    head_limit = jnp.sum(jnp.where(jnp.arange(pieces) == row_index, piece_heads, 0))
    unit_limit = jnp.sum(jnp.where(jnp.arange(pieces) == row_index, piece_ffn, 0))
    head_mask = (model_index * local_heads + jnp.arange(local_heads) < head_limit).astype(
        jnp.float32
    )
    unit_mask = (model_index * local_units + jnp.arange(local_units) < unit_limit).astype(
        jnp.float32
    )
    positions = jnp.arange(tgt_slots)
    self_mask = (positions[None, :, None] >= positions[None, None, :]) & (
        positions[None, None, :] < tgt_len[:, None, None]
    )
    cross_mask = jnp.broadcast_to(
        jnp.arange(src_slots)[None, None, :] < src_len[:, None, None],
        (seq_count, tgt_slots, src_slots),
    )
    head_scale = head_mask[None, None, :, None]

    def heads_of(values, length):
        return values.reshape(seq_count, length, local_heads, HD)

    stacked = encoder.reshape(row_count, seq_count * src_slots, model_width)
    layers_in = lax.all_to_all(stacked, "row", split_axis=0, concat_axis=0, tiled=True)
    memory = jnp.sum(own_weight[:, None, None] * layers_in.astype(jnp.float32), axis=0)
    memory_low = memory.astype(jnp.bfloat16)
    stream_in = tokens.astype(jnp.float32)
    normed_one = layer_norm(stream_in, norm_gain[0], norm_shift[0]).astype(jnp.bfloat16)
    proj_one = jnp.einsum("td,cde->cte", normed_one, w_self, preferred_element_type=jnp.float32)
    query_one = heads_of((proj_one[0] + b_self[0]).astype(jnp.bfloat16), tgt_slots)
    key_one = heads_of(proj_one[1].astype(jnp.bfloat16), tgt_slots)
    value_one = heads_of((proj_one[2] + b_self[1]).astype(jnp.bfloat16), tgt_slots)
    mixed_one, log_one = attend_forward(query_one, key_one, value_one, self_mask)
    attn_one = (mixed_one * head_scale).astype(jnp.bfloat16).reshape(tokens_count, -1)
    branch_one = lax.psum(jnp.dot(attn_one, o_self, preferred_element_type=jnp.float32), "mp")
    stream_mid = stream_in + branch_one + out_bias[0]
    normed_two = layer_norm(stream_mid, norm_gain[1], norm_shift[1]).astype(jnp.bfloat16)
    query_two = heads_of(
        (jnp.dot(normed_two, w_cross[0], preferred_element_type=jnp.float32) + b_cross[0]).astype(
            jnp.bfloat16
        ),
        tgt_slots,
    )
    proj_two = jnp.einsum(
        "sd,cde->cse", memory_low, w_cross[1:], preferred_element_type=jnp.float32
    )
    key_two = heads_of(proj_two[0].astype(jnp.bfloat16), src_slots)
    value_two = heads_of((proj_two[1] + b_cross[1]).astype(jnp.bfloat16), src_slots)
    mixed_two, log_two = attend_forward(query_two, key_two, value_two, cross_mask)
    attn_two = (mixed_two * head_scale).astype(jnp.bfloat16).reshape(tokens_count, -1)
    branch_two = lax.psum(jnp.dot(attn_two, o_cross, preferred_element_type=jnp.float32), "mp")
    stream_late = stream_mid + branch_two + out_bias[1]
    normed_three = layer_norm(stream_late, norm_gain[2], norm_shift[2]).astype(jnp.bfloat16)
    hidden = jnp.dot(normed_three, w_up, preferred_element_type=jnp.float32) + b_up
    activated, gelu_pull = jax.vjp(jax.nn.gelu, hidden)
    active = (activated * unit_mask).astype(jnp.bfloat16)
    branch_three = lax.psum(jnp.dot(active, w_down, preferred_element_type=jnp.float32), "mp")
    block_out = stream_late + branch_three + out_bias[2]
    grad_out = cotangent.astype(jnp.float32)
    bias_three = column_sum(cotangent)
    grad_w_down = jnp.dot(active.T, cotangent, preferred_element_type=jnp.float32)
    grad_active = jnp.dot(cotangent, w_down.T, preferred_element_type=jnp.float32) * unit_mask
    grad_hidden = gelu_pull(grad_active)[0].astype(jnp.bfloat16)
    grad_b_up = column_sum(grad_hidden)
    grad_w_up = jnp.dot(normed_three.T, grad_hidden, preferred_element_type=jnp.float32)
    grad_normed_three = lax.psum(
        jnp.dot(grad_hidden, w_up.T, preferred_element_type=jnp.float32), "mp"
    )
    back_three, gain_three, shift_three = norm_back(
        stream_late, norm_gain[2], norm_shift[2], grad_normed_three
    )
    grad_late = grad_out + back_three
    late_low = grad_late.astype(jnp.bfloat16)
    bias_two = column_sum(late_low)
    grad_o_cross = jnp.dot(attn_two.T, late_low, preferred_element_type=jnp.float32)
    heads_grad_two = (
        heads_of(jnp.dot(late_low, o_cross.T, preferred_element_type=jnp.float32), tgt_slots)
        * head_scale
    ).astype(jnp.bfloat16)
    query_grad_two, key_grad_two, value_grad_two = attend_backward(
        query_two, key_two, value_two, cross_mask, log_two, heads_grad_two
    )
    query_grad_two = query_grad_two.reshape(tokens_count, -1).astype(jnp.bfloat16)
    key_grad_two = key_grad_two.reshape(seq_count * src_slots, -1).astype(jnp.bfloat16)
    value_grad_two = value_grad_two.reshape(seq_count * src_slots, -1).astype(jnp.bfloat16)
    grad_b_cross = jnp.stack([column_sum(query_grad_two), column_sum(value_grad_two)])
    grad_w_cross = jnp.stack(
        [
            jnp.dot(normed_two.T, query_grad_two, preferred_element_type=jnp.float32),
            jnp.dot(memory_low.T, key_grad_two, preferred_element_type=jnp.float32),
            jnp.dot(memory_low.T, value_grad_two, preferred_element_type=jnp.float32),
        ]
    )
    normed_part_two = jnp.dot(query_grad_two, w_cross[0].T, preferred_element_type=jnp.float32)
    memory_part = jnp.dot(key_grad_two, w_cross[1].T, preferred_element_type=jnp.float32) + jnp.dot(
        value_grad_two, w_cross[2].T, preferred_element_type=jnp.float32
    )
    grad_normed_two, grad_memory = lax.psum((normed_part_two, memory_part), "mp")
    spread_back = own_weight[:, None, None] * grad_memory[None]
    grad_encoder = lax.all_to_all(spread_back, "row", split_axis=0, concat_axis=0, tiled=True)
    grad_encoder = grad_encoder.reshape(1, row_count * seq_count * src_slots, model_width)
    back_two, gain_two, shift_two = norm_back(
        stream_mid, norm_gain[1], norm_shift[1], grad_normed_two
    )
    grad_mid = grad_late + back_two
    mid_low = grad_mid.astype(jnp.bfloat16)
    bias_one = column_sum(mid_low)
    grad_o_self = jnp.dot(attn_one.T, mid_low, preferred_element_type=jnp.float32)
    heads_grad_one = (
        heads_of(jnp.dot(mid_low, o_self.T, preferred_element_type=jnp.float32), tgt_slots)
        * head_scale
    ).astype(jnp.bfloat16)
    query_grad_one, key_grad_one, value_grad_one = attend_backward(
        query_one, key_one, value_one, self_mask, log_one, heads_grad_one
    )
    query_grad_one = query_grad_one.reshape(tokens_count, -1).astype(jnp.bfloat16)
    key_grad_one = key_grad_one.reshape(tokens_count, -1).astype(jnp.bfloat16)
    value_grad_one = value_grad_one.reshape(tokens_count, -1).astype(jnp.bfloat16)
    grad_b_self = jnp.stack([column_sum(query_grad_one), column_sum(value_grad_one)])
    stacked_grads = jnp.stack([query_grad_one, key_grad_one, value_grad_one])
    grad_w_self = jnp.einsum(
        "td,cte->cde", normed_one, stacked_grads, preferred_element_type=jnp.float32
    )
    normed_part_one = jnp.einsum(
        "cte,cde->td", stacked_grads, w_self, preferred_element_type=jnp.float32
    )
    grad_normed_one = lax.psum(normed_part_one, "mp")
    back_one, gain_one, shift_one = norm_back(
        stream_in, norm_gain[0], norm_shift[0], grad_normed_one
    )
    grad_tokens = grad_mid + back_one
    grad_gain = jnp.stack([gain_one, gain_two, gain_three])
    grad_shift = jnp.stack([shift_one, shift_two, shift_three])
    grad_bias_out = jnp.stack([bias_one, bias_two, bias_three])
    sum_b_self, sum_b_cross, sum_b_up = lax.psum(
        (grad_b_self, grad_b_cross, grad_b_up), ("row", "dp")
    )
    (
        shard_gain,
        shard_shift,
        shard_bias,
        shard_w_self,
        shard_o_self,
        shard_w_cross,
        shard_o_cross,
        shard_w_up,
        shard_w_down,
    ) = (
        lax.psum_scatter(grad_gain, ("row", "dp"), scatter_dimension=1, tiled=True),
        lax.psum_scatter(grad_shift, ("row", "dp"), scatter_dimension=1, tiled=True),
        lax.psum_scatter(grad_bias_out, ("row", "dp"), scatter_dimension=1, tiled=True),
        lax.psum_scatter(grad_w_self, ("row", "dp"), scatter_dimension=1, tiled=True),
        lax.psum_scatter(grad_o_self, ("row", "dp"), scatter_dimension=1, tiled=True),
        lax.psum_scatter(grad_w_cross, ("row", "dp"), scatter_dimension=1, tiled=True),
        lax.psum_scatter(grad_o_cross, ("row", "dp"), scatter_dimension=1, tiled=True),
        lax.psum_scatter(grad_w_up, ("row", "dp"), scatter_dimension=0, tiled=True),
        lax.psum_scatter(grad_w_down, ("row", "dp"), scatter_dimension=1, tiled=True),
    )
    return (
        block_out,
        grad_tokens,
        grad_encoder,
        shard_gain,
        shard_shift,
        shard_bias,
        shard_w_self,
        shard_o_self,
        sum_b_self,
        shard_w_cross,
        shard_o_cross,
        sum_b_cross,
        shard_w_up,
        sum_b_up,
        shard_w_down,
    )


def solution(mesh):
    return jax.shard_map(
        per_device,
        mesh=mesh,
        in_specs=(
            P(("row", "dp"), None),
            P("row", "dp", None),
            P(),
            P(),
            P(),
            P(("row", "dp")),
            P(("row", "dp")),
            P(),
            P(),
            P(),
            P(None, None, "mp"),
            P("mp", None),
            P(None, "mp"),
            P(None, None, "mp"),
            P("mp", None),
            P(None, "mp"),
            P(None, "mp"),
            P("mp"),
            P("mp", None),
            P(("row", "dp"), None),
        ),
        out_specs=(
            P(("row", "dp"), None),
            P(("row", "dp"), None),
            P("row", "dp", None),
            P(None, ("row", "dp")),
            P(None, ("row", "dp")),
            P(None, ("row", "dp")),
            P(None, ("row", "dp"), "mp"),
            P("mp", ("row", "dp")),
            P(None, "mp"),
            P(None, ("row", "dp"), "mp"),
            P("mp", ("row", "dp")),
            P(None, "mp"),
            P(("row", "dp"), "mp"),
            P("mp"),
            P("mp", ("row", "dp")),
        ),
        check_vma=False,
    )
```

profile of v0, /device:TPU:0, one launch (start us, length us, event | category | flops | bytes accessed | tf_op | source)
XLA Modules:
  0.0 1376.4 jit_solution(3262438363548629721)
XLA Ops:
  7.2 6.6 all-to-all-start
  15.0 3.2 convolution_bitcast_fusion
  23.5 3.5 fusion.169
  27.0 2.8 squeeze.21
  29.8 2.8 squeeze.22
  34.2 2.7 fusion.170
  44.9 23.3 %all-reduce.17.cloned.1.call-done = f32[1024,640]{1,0:T(8,128)} async-done(((f32[1024,640]{1,0:T(8,128)}), f32[1024,640]{1,0:T(8,128)}) %all-reduce.17.cloned.1.call-update) | async-done | bytes 2621456 | tf_op jit(solution)/shard_map/psum | solution.py:140
  73.0 2.5 fusion.68
  78.0 51.9 %all-to-all-done = bf16[4,1024,640]{2,1,0:T(8,128)(2,1)} async-done(((bf16[4,1024,640]{2,1,0:T(8,128)(2,1)}), bf16[4,1024,640]{2,1,0:T(8,128)(2,1)}, u32[]{:S(2)}, u32[]{:S(2)}) %all-to-all-start) | async-done | bytes 5242912 | tf_op jit(solution)/shard_map/all_to_all | solution.py:129
  129.9 3.7 multiply_reduce_fusion
  137.0 2.8 squeeze.23
  153.6 19.9 %all-reduce.19.cloned.1.call-done = f32[1024,640]{1,0:T(8,128)} async-done(((f32[1024,640]{1,0:T(8,128)}), f32[1024,640]{1,0:T(8,128)}) %all-reduce.19.cloned.1.call-update) | async-done | bytes 2621456 | tf_op jit(solution)/shard_map/psum | solution.py:156
  173.4 2.9 fusion.166
  177.1 5.4 multiply_convert_fusion
  182.5 7.0 convert_reduce_fusion
  191.2 4.1 fusion.179
  195.6 23.2 %all-reduce.21.cloned.1.call-done = f32[1024,640]{1,0:T(8,128)} async-done(((f32[1024,640]{1,0:T(8,128)}), f32[1024,640]{1,0:T(8,128)}) %all-reduce.21.cloned.1.call-update) | async-done | bytes 2621456 | tf_op jit(solution)/shard_map/psum | solution.py:171
  218.8 3.6 multiply_reduce_fusion.3
  230.4 4.4 fusion.132
  234.8 8.6 convert_reduce_fusion.6
  245.1 3.4 fusion.118
  249.1 6.7 fusion.178
  257.5 8.5 fusion.99
  272.1 3.6 multiply_reduce_fusion.4
  284.1 4.5 fusion.127
  290.3 9.0 fusion.105
  299.3 8.6 convert_reduce_fusion.8
  317.5 2.6 convert_element_type.272
  322.8 3.4 convolution_bitcast_fusion.2
  332.3 6.3 copy.113
  338.6 3.4 convolution_bitcast_fusion.3
  341.9 5.6 copy.112
  348.9 3.0 fusion.181
  351.9 4.2 fusion.144
  356.1 6.6 all-reduce.27.cloned.1.call-done
  362.7 6.6 broadcast_multiply_fusion
  369.3 6.0 all-to-all-start.1
  375.4 8.1 fusion.160
  384.7 6.0 fusion.182
  393.1 433.1 %all-reduce.25.cloned.1.call-done = (f32[3,640,320]{2,0,1:T(4,128)}, f32[3,640,320]{2,0,1:T(4,128)}) async-done(((f32[3,640,320]{2,0,1:T(4,128)}, f32[3,640,320]{2,0,1:T(4,128)}), (f32[3,640,320]{2,0,1:T(4,128)}, f32[3,640,320]{2,0,1:T(4,128)})) %all-reduce.25.cloned.1.call-update) | async-done | bytes 4915216
  829.7 2.6 fusion.162
  833.9 75.7 %all-reduce.7 = (f32[3,640]{1,0:T(4,128)S(1)}, f32[3,640]{1,0:T(4,128)S(1)}, f32[3,640]{1,0:T(4,128)S(1)}, f32[2,320]{1,0:T(2,128)}, f32[2,320]{1,0:T(2,128)}, /*index=5*/f32[1536]{0:T(1024)}) all-reduce(f32[3,640]{1,0:T(4,128)S(1)} %pad_maximum_fusion.1, ...), channel_id=2, replica_groups=mesh['row'=4,'dp'=4,'mp'=2] {'row','dp'}, use_global_device_ids=true, to_apply=%region_33.34.clone | all-reduce | flops 8576 | bytes 68608
  911.5 4.4 add_add_fusion.5
  918.3 35.6 %reduce-scatter.18.cloned.1.call-done = f32[320,40]{0,1:T(8,128)} async-done(((f32[320,640]{0,1:T(8,128)}), f32[320,40]{0,1:T(8,128)}) %reduce-scatter.18.cloned.1.call-update) | async-done | bytes 51216
  953.9 127.7 %reduce-scatter.16.cloned.1.call-done = f32[320,40]{0,1:T(8,128)} async-done(((f32[320,640]{0,1:T(8,128)}), f32[320,40]{0,1:T(8,128)}) %reduce-scatter.16.cloned.1.call-update) | async-done | bytes 51216
  1081.6 139.2 %reduce-scatter.12.cloned.1.call-done = f32[40,1536]{1,0:T(8,128)} async-done(((f32[640,1536]{1,0:T(8,128)}), f32[40,1536]{1,0:T(8,128)}) %reduce-scatter.12.cloned.1.call-update) | async-done | bytes 245776 | tf_op jit(solution)/shard_map/reduce_scatter | solution.py:261
  1220.9 139.4 %reduce-scatter.14.cloned.1.call-done = f32[1536,40]{0,1:T(8,128)} async-done(((f32[1536,640]{0,1:T(8,128)}), f32[1536,40]{0,1:T(8,128)}) %reduce-scatter.14.cloned.1.call-update) | async-done | bytes 245776 | tf_op jit(solution)/shard_map/reduce_scatter | solution.py:262
  1360.2 8.9 copy.200
  (268 shorter events, 102.8 us)
Async XLA Ops:
  7.2 169.6 %copy-start = (bf16[640,1536]{1,0:T(8,128)(2,1)S(1)}, bf16[640,1536]{1,0:T(8,128)(2,1)}, u32[]{:S(2)}) copy-start(bf16[640,1536]{1,0:T(8,128)(2,1)} %param.36) | copy-start | bytes 5898244
  7.2 6.7 copy-start.6
  7.2 122.7 %all-to-all-start = ((bf16[4,1024,640]{2,1,0:T(8,128)(2,1)}), bf16[4,1024,640]{2,1,0:T(8,128)(2,1)}, u32[]{:S(2)}, u32[]{:S(2)}) async-start(bf16[4,1024,640]{2,1,0:T(8,128)(2,1)} %bitcast.150), calls=%async_computation | async-start | bytes 10485760 | tf_op jit(solution)/shard_map/all_to_all | solution.py:129
  13.8 54.4 %all-reduce.17.cloned.1.call-start = ((), (), s32[]{:S(2)}) async-start(), calls=%async_computation.6 | async-start | bytes 5242880 | tf_op jit(solution)/shard_map/psum | solution.py:140
  14.7 3.5 copy-start.50
  27.0 5.6 copy-start.61
  27.0 6.9 copy-start.62
  36.9 3.3 copy-start.9
  41.8 2.7 copy-start.57
  41.8 2.8 copy-start.52
  41.8 3.0 copy-start.55
  41.8 3.1 copy-start.63
  44.3 129.2 %all-reduce.19.cloned.1.call-start = ((), (), s32[]{:S(2)}) async-start(), calls=%async_computation.7 | async-start | bytes 5242880 | tf_op jit(solution)/shard_map/psum | solution.py:156
  129.9 3.7 copy-start.45
  144.7 3.3 copy-start.15
  149.5 2.7 copy-start.64
  152.0 66.8 %all-reduce.21.cloned.1.call-start = ((), (), s32[]{:S(2)}) async-start(), calls=%async_computation.8 | async-start | bytes 5242880 | tf_op jit(solution)/shard_map/psum | solution.py:171
  176.3 6.2 copy-start.4
  177.1 5.4 copy-start.26
  177.1 5.4 copy-start.58
  195.3 76.8 %all-reduce.23.cloned.1.call-start = ((), (), s32[]{:S(2)}) async-start(), calls=%async_computation.9 | async-start | bytes 5242880 | tf_op jit(solution)/shard_map/psum | solution.py:203
  218.8 3.6 copy-start.5
  218.8 4.1 copy-start.20
  230.4 4.4 copy-start.47
  248.6 114.2 %all-reduce.27.cloned.1.call-start = ((), (), s32[]{:S(2)}) async-start(), calls=%async_computation.15 | async-start | bytes 15728640 | tf_op jit(solution)/shard_map/psum | solution.py:162
  249.1 6.7 copy-start.16
  257.5 10.8 copy-start.21
  266.6 4.2 copy-start.22
  272.1 3.6 copy-start.3
  272.1 4.1 copy-start.19
  284.1 4.5 copy-start.10
  290.3 9.0 copy-start.38
  299.3 8.6 copy-start.40
  320.1 2.7 copy-start.59
  326.1 500.0 %all-reduce.25.cloned.1.call-start = ((), (), s32[]{:S(2)}) async-start(), calls=%async_computation.14 | async-start | bytes 15728640
  327.4 2.6 copy-start.35
  332.3 6.3 copy-start.49
  347.6 4.3 copy-start.25
  347.6 606.3 %reduce-scatter.18.cloned.1.call-start = ((), (), s32[]{:S(2)}) async-start(), calls=%async_computation.13 | async-start | bytes 1044480
  351.9 729.8 %reduce-scatter.16.cloned.1.call-start = ((), (), s32[]{:S(2)}) async-start(), calls=%async_computation.12 | async-start | bytes 1044480
  369.3 549.0 %all-to-all-start.1 = ((f32[4,1024,640]{2,1,0:T(8,128)}), f32[4,1024,640]{2,1,0:T(8,128)}, u32[]{:S(2)}, u32[]{:S(2)}) async-start(f32[4,1024,640]{2,1,0:T(8,128)} %broadcast_multiply_fusion), calls=%async_computation.1 | async-start | bytes 20971520 | tf_op jit(solution)/shard_map/all_to_all | solution.py:205
  375.3 845.5 %reduce-scatter.12.cloned.1.call-start = ((), (), s32[]{:S(2)}) async-start(), calls=%async_computation.10 | async-start | bytes 4177920 | tf_op jit(solution)/shard_map/reduce_scatter | solution.py:261
  383.4 976.8 %reduce-scatter.14.cloned.1.call-start = ((), (), s32[]{:S(2)}) async-start(), calls=%async_computation.11 | async-start | bytes 4177920 | tf_op jit(solution)/shard_map/reduce_scatter | solution.py:262
  827.2 5.1 copy-start.51
  827.2 5.2 copy-start.13
  911.5 4.4 copy-start.8
  911.5 4.6 copy-start.14
  1360.2 8.9 copy-start.1
  (30 other events, 44.4 us)
Sparse Core Ops, SparseCore 0:
  44.4 23.7 all-reduce.16
  152.1 21.2 all-reduce.18
  195.4 23.3 all-reduce.20
  248.7 23.3 all-reduce.22
  326.3 36.4 all-reduce.26
  370.2 455.9 all-reduce.24
  831.5 122.3 reduce-scatter.17
  959.2 122.3 reduce-scatter.15
  1087.3 133.5 reduce-scatter.11
  1226.4 133.8 reduce-scatter.13
where the time goes:
time: 1390 us; the launch traced here: 1380 us
  waiting for transfers between devices  1000 us (72%)
  matrix products  130 us (9%)
  local copies, waits for them, and re-layouts  93.3 us (7%)
  blocking collectives  75.7 us (5%)
  other arithmetic  45.4 us (3%)
  between operations  16.3 us (1%)
  starting transfers between devices  14.4 us (1%)
    unnamed x13, waiting for transfers between devices  597 us
    reduce_scatter x1, waiting for transfers between devices, per_device(): lax.psum_scatter(grad_w_down, ('row', 'dp'), scatter_dimension=1, tiled=T...  139 us
    reduce_scatter x1, waiting for transfers between devices, per_device(): lax.psum_scatter(grad_w_up, ('row', 'dp'), scatter_dimension=0, tiled=True)  139 us
    unnamed x1, blocking collectives  75.7 us
    all_to_all x1, waiting for transfers between devices, per_device(): lax.all_to_all(stacked, 'row', split_axis=0, concat_axis=0, tiled=True)  51.9 us
    unnamed x148, local copies, waits for them, and re-layouts  38.7 us
  transfers between devices with their start and end apart: 12, of which 11 were waited for; matrix products, arithmetic and copies ran while one was open for 9% of the time, Pallas kernels for 0%

commit v1 on v0

v1 whole, which is shorter than its diff:
```python
import functools
import jax
import jax.numpy as jnp
from jax import lax
from jax.experimental import pallas as pl
from jax.experimental.pallas import tpu as pltpu
from jax.sharding import PartitionSpec as P

HD = 80
EPSILON = 1e-05
MASKED = -1e30
F32, BF16 = jnp.float32, jnp.bfloat16
MESH = pl.DeviceIdType.MESH
ANY = pl.BlockSpec(memory_space=pl.ANY)
VMEM = pl.BlockSpec(memory_space=pltpu.VMEM)


def nn(a, b):
    return lax.dot_general(a, b, (((1,), (0,)), ((), ())), preferred_element_type=F32)


def nt(a, b):
    return lax.dot_general(a, b, (((1,), (1,)), ((), ())), preferred_element_type=F32)


def tn(a, b):
    return lax.dot_general(a, b, (((0,), (0,)), ((), ())), preferred_element_type=F32)


def lanes(i, n):
    return pl.ds(pl.multiple_of(i * n, n), n)


def layer_norm(v_ref, x_ref, gain, shift):
    @pl.loop(0, v_ref.shape[1] // 128)
    def _(i):
        v = v_ref[:, lanes(i, 128)].astype(F32)
        c = v - jnp.mean(v, axis=0, keepdims=True)
        r = lax.rsqrt(jnp.mean(c * c, axis=0, keepdims=True) + EPSILON)
        x_ref[:, lanes(i, 128)] = (c * r * gain + shift).astype(BF16)


def norm_back(v_ref, gain, up_ref, base_ref, out_ref, low_ref, gain_sum, shift_sum, bias_sum):
    for ref in (gain_sum, shift_sum, bias_sum):
        if ref is not None:
            ref[...] = jnp.zeros_like(ref)

    @pl.loop(0, v_ref.shape[1] // 128)
    def _(i):
        at = lanes(i, 128)
        v = v_ref[:, at].astype(F32)
        c = v - jnp.mean(v, axis=0, keepdims=True)
        r = lax.rsqrt(jnp.mean(c * c, axis=0, keepdims=True) + EPSILON)
        xhat = c * r
        e = up_ref[:, at]
        gain_sum[...] += e * xhat
        shift_sum[...] += e
        eg = e * gain
        m1 = jnp.mean(eg, axis=0, keepdims=True)
        m2 = jnp.mean(eg * xhat, axis=0, keepdims=True)
        out = base_ref[:, at].astype(F32) + r * (eg - m1 - xhat * m2)
        out_ref[:, at] = out
        if low_ref is not None:
            low = out.astype(BF16)
            low_ref[:, at] = low
            bias_sum[...] += low.astype(F32)


def attend(q_ref, k_ref, v_ref, out_ref, out_row, prob_ref, masks, head_on, hd, heads):
    groups, slots = len(out_row), masks[0].shape[1]
    per = heads // groups
    for g in range(groups):

        @pl.loop(0, per)
        def _(h, g=g):
            rows = pl.ds(pl.multiple_of((g * per + h) * hd, 16), hd)
            to = pl.ds(pl.multiple_of(out_row[g] + h * hd, 16), hd)
            for s, mask in enumerate(masks):
                at = slice(s * slots, (s + 1) * slots)
                scores = tn(k_ref[rows, at], q_ref[rows, at]) * hd ** (-0.5)
                scores = jnp.where(mask, scores, MASKED)
                e = jnp.exp(scores - jnp.max(scores, axis=0, keepdims=True))
                total = jnp.sum(e, axis=0, keepdims=True)
                p = (e / total).astype(BF16)
                prob_ref[(g * per + h) * len(masks) + s] = p
                mixed = nn(v_ref[rows, at], p) * head_on[g * per + h]
                out_ref[g, to, at] = mixed.astype(BF16)


def attend_back(q_ref, k_ref, v_ref, e_ref, prob_ref, d_ref, at_rows, hd, heads, sents):
    groups = d_ref.shape[0]
    per, slots = heads // groups, q_ref.shape[1] // sents
    for g in range(groups):

        @pl.loop(0, per)
        def _(h, g=g):
            rows = pl.ds(pl.multiple_of((g * per + h) * hd, 16), hd)
            dq_at, dk_at, dv_at = [
                pl.ds(pl.multiple_of(first + h * hd, 16), hd) for first in at_rows
            ]
            for s in range(sents):
                at = slice(s * slots, (s + 1) * slots)
                e, p = e_ref[rows, at], prob_ref[(g * per + h) * sents + s]
                d_ref[g, dv_at, at] = nt(e, p).astype(BF16)
                dp = tn(v_ref[rows, at], e)
                pf = p.astype(F32)
                delta = jnp.sum(pf * dp, axis=0, keepdims=True)
                ds = (pf * (dp - delta) * hd ** (-0.5)).astype(BF16)
                d_ref[g, dq_at, at] = nn(k_ref[rows, at], ds).astype(BF16)
                d_ref[g, dk_at, at] = nt(q_ref[rows, at], ds).astype(BF16)


def lane_sum(values):
    return jnp.sum(values.astype(F32), axis=1, keepdims=True)


def compute_kernel(
    hd, lw, head_on, ints, tok, cot, enc, ws, os_, wc, oc, wu, wd, cols, bcols, bup,
    block, gtok, gmem, gs, gx, gu, gd, small,
    tok_t, mid_t, late_t, acc_a, acc_b, x1, x2, x3, ct, mem_t, e_low,
    q1, k1, v1, q2, k2, v2, attn1, attn2, prob1, prob2, grads, eh, sum_a, sum_b, sum_c, vec, bvec, ubias,
    wu_buf, wd_buf, gu_buf, gd_buf, in_sem, out_sem,
):
    width, tokens = tok_t.shape
    groups, hw = ws.shape[0], ws.shape[3]
    heads, units = groups * hw // hd, wu.shape[2]
    sents = ints.shape[0] - 1 >> 1
    slots = tokens // sents
    pad = -(-3 * hw // 128) * 128
    lead = 3 * hw // 128 * 128
    first = 3 * hw - lead
    gain = [cols[:, i : i + 1] for i in range(3)]
    shift = [cols[:, 3 + i : 4 + i] for i in range(3)]
    obias = [cols[:, 6 + i : 7 + i] for i in range(3)]
    key_at = lax.broadcasted_iota(jnp.int32, (slots, slots), 0)
    query_at = lax.broadcasted_iota(jnp.int32, (slots, slots), 1)
    for ref in (attn1, attn2):
        ref[:, :first, :] = jnp.zeros((groups, first, tokens), BF16)
    grads[:, 3 * hw :, :] = jnp.zeros((groups, pad - 3 * hw, tokens), BF16)

    vec[...] = jnp.zeros_like(vec)
    bvec[...] = jnp.zeros_like(bvec)

    tok_t[...] = tok[...].astype(F32).T.astype(BF16)
    layer_norm(tok_t, x1, gain[0], shift[0])
    for g in range(groups):
        rows = slice(g * hw, (g + 1) * hw)
        q1[rows] = (tn(ws[g, 0], x1[...]) + bcols[g, :, 0:1]).astype(BF16)
        k1[rows] = tn(ws[g, 1], x1[...]).astype(BF16)
        v1[rows] = (tn(ws[g, 2], x1[...]) + bcols[g, :, 1:2]).astype(BF16)
    masks = [(key_at <= query_at) & (key_at < ints[1 + s]) for s in range(sents)]
    attend(q1, k1, v1, attn1, [first] * groups, prob1, masks, head_on, hd, heads)
    acc_a[...] = tn(os_[0], attn1[0, first:])
    for g in range(1, groups):
        acc_a[...] += tn(os_[g], attn1[g, first:])
    mid_t[...] = tok_t[...].astype(F32) + acc_a[...] + obias[0]

    memory = lw[0] * enc[0].astype(F32)
    for i in range(1, enc.shape[0]):
        memory += lw[i] * enc[i].astype(F32)
    mem_t[...] = memory.T.astype(BF16)
    layer_norm(mid_t, x2, gain[1], shift[1])
    for g in range(groups):
        rows = slice(g * hw, (g + 1) * hw)
        q2[rows] = (tn(wc[g, 0], x2[...]) + bcols[g, :, 2:3]).astype(BF16)
        k2[rows] = tn(wc[g, 1], mem_t[...]).astype(BF16)
        v2[rows] = (tn(wc[g, 2], mem_t[...]) + bcols[g, :, 3:4]).astype(BF16)
    masks = [key_at < ints[1 + sents + s] for s in range(sents)]
    attend(q2, k2, v2, attn2, [first] * groups, prob2, masks, head_on, hd, heads)
    acc_a[...] = tn(oc[0], attn2[0, first:])
    for g in range(1, groups):
        acc_a[...] += tn(oc[g], attn2[g, first:])
    late_t[...] = mid_t[...] + acc_a[...] + obias[1]

    layer_norm(late_t, x3, gain[2], shift[2])
    ct[...] = cot[...].astype(F32).T.astype(BF16)
    acc_a[...] = jnp.zeros_like(acc_a)
    acc_b[...] = jnp.zeros_like(acc_b)
    ubias[...] = jnp.zeros_like(ubias)
    ublk = bup.shape[1]
    blocks = units // ublk

    def fetches(i):
        slot, g, at = lax.rem(i, 2), i // blocks, lanes(lax.rem(i, blocks), ublk)
        return [
            pltpu.make_async_copy(wu.at[g, :, at], wu_buf.at[slot], in_sem.at[0, slot]),
            pltpu.make_async_copy(wd.at[g, at, :], wd_buf.at[slot], in_sem.at[1, slot]),
        ]

    def writes(i):
        slot, g, at = lax.rem(i, 2), i // blocks, lanes(lax.rem(i, blocks), ublk)
        return [
            pltpu.make_async_copy(gu_buf.at[slot], gu.at[g, :, at], out_sem.at[0, slot]),
            pltpu.make_async_copy(gd_buf.at[slot], gd.at[g, :, at], out_sem.at[1, slot]),
        ]

    for copy in fetches(0):
        copy.start()

    @pl.loop(0, groups * blocks)
    def _(i):
        slot, g = lax.rem(i, 2), i // blocks
        outs = writes(i)

        @pl.when(i + 1 < groups * blocks)
        def _():
            for copy in fetches(i + 1):
                copy.start()

        for copy in fetches(i):
            copy.wait()
        up, down = wu_buf.at[slot], wd_buf.at[slot]
        mine = lax.broadcasted_iota(jnp.int32, (ublk, 128), 1) == lax.rem(i, blocks)
        h = tn(up[...], x3[...]) + lane_sum(jnp.where(mine, bup[g], 0.0))
        unit = i * ublk + lax.broadcasted_iota(jnp.int32, (ublk, 1), 0)
        on = jnp.where(unit < ints[0], 1.0, 0.0)
        inner = 0.7978845608028654 * (h + 0.044715 * (h * h * h))
        t = jnp.tanh(inner)
        cdf = 0.5 * (1.0 + t)
        slope = cdf + 0.5 * h * (1.0 - t * t) * (
            0.7978845608028654 * (1.0 + 3 * 0.044715 * h * h)
        )
        act = (h * cdf * on).astype(BF16)
        acc_a[...] += tn(down[...], act)
        dh = (nn(down[...], ct[...]) * slope * on).astype(BF16)
        ubias[g] += jnp.where(mine, lane_sum(dh), 0.0)
        acc_b[...] += nn(up[...], dh)

        @pl.when(i >= 2)
        def _():
            for copy in writes(i - 2):
                copy.wait()

        gu_buf[slot] = nt(x3[...], dh).astype(BF16)
        gd_buf[slot] = nt(ct[...], act).astype(BF16)
        for copy in outs:
            copy.start()

    for i in (groups * blocks - 2, groups * blocks - 1):
        for copy in writes(i):
            copy.wait()
    block[...] = (late_t[...] + acc_a[...] + obias[2]).T
    vec[:, 8:9] = lane_sum(ct[...])
    norm_back(late_t, gain[2], acc_b, ct, acc_a, e_low, sum_a, sum_b, sum_c)
    vec[:, 2:3] = lane_sum(sum_a[...])
    vec[:, 5:6] = lane_sum(sum_b[...])
    vec[:, 7:8] = lane_sum(sum_c[...])

    for g in range(groups):
        for h in range(hw // hd):
            rows = slice(h * hd, (h + 1) * hd)
            eh[g * hw + h * hd : g * hw + (h + 1) * hd] = (
                nn(oc[g, rows], e_low[...]) * head_on[g * (hw // hd) + h]
            ).astype(BF16)
    attend_back(q2, k2, v2, eh, prob2, grads, (2 * hw, 0, hw), hd, heads, sents)
    for g in range(groups):
        bvec[g, :, 2:3] = lane_sum(grads[g, 2 * hw : 3 * hw])
        bvec[g, :, 3:4] = lane_sum(grads[g, hw : 2 * hw])

        @pl.loop(0, 2 * hw // 128)
        def _(i, g=g):
            gx[g, :, lanes(i, 128)] = nt(mem_t[...], grads[g, lanes(i, 128)]).astype(BF16)

        @pl.loop(2 * hw // 128, lead // 128)
        def _(i, g=g):
            gx[g, :, lanes(i, 128)] = nt(x2[...], grads[g, lanes(i, 128)]).astype(BF16)

        tail = nt(e_low[...], attn2[g])
        gx[g, :, lead:pad] = (tail[:, :128] + nt(x2[...], grads[g, lead:pad])).astype(BF16)
        gx[g, :, pad:] = tail[:, 128:].astype(BF16)
        part = nn(wc[g, 0], grads[g, 2 * hw : 3 * hw])
        mpart = nn(wc[g, 1], grads[g, :hw]) + nn(wc[g, 2], grads[g, hw : 2 * hw])
        if g == 0:
            acc_b[...] = part
            tok_m = mpart
        else:
            acc_b[...] += part
            tok_m += mpart
    gmem[...] = tok_m.T.astype(BF16)
    norm_back(mid_t, gain[1], acc_b, acc_a, acc_a, e_low, sum_a, sum_b, sum_c)
    vec[:, 1:2] = lane_sum(sum_a[...])
    vec[:, 4:5] = lane_sum(sum_b[...])
    vec[:, 6:7] = lane_sum(sum_c[...])

    for g in range(groups):
        for h in range(hw // hd):
            rows = slice(h * hd, (h + 1) * hd)
            eh[g * hw + h * hd : g * hw + (h + 1) * hd] = (
                nn(os_[g, rows], e_low[...]) * head_on[g * (hw // hd) + h]
            ).astype(BF16)
    attend_back(q1, k1, v1, eh, prob1, grads, (0, hw, 2 * hw), hd, heads, sents)
    for g in range(groups):
        bvec[g, :, 0:1] = lane_sum(grads[g, :hw])
        bvec[g, :, 1:2] = lane_sum(grads[g, 2 * hw : 3 * hw])

        @pl.loop(0, lead // 128)
        def _(i, g=g):
            gs[g, :, lanes(i, 128)] = nt(x1[...], grads[g, lanes(i, 128)]).astype(BF16)

        tail = nt(e_low[...], attn1[g])
        gs[g, :, lead:pad] = (tail[:, :128] + nt(x1[...], grads[g, lead:pad])).astype(BF16)
        gs[g, :, pad:] = tail[:, 128:].astype(BF16)
        for j in range(3):
            part = nn(ws[g, j], grads[g, j * hw : (j + 1) * hw])
            if g == 0 and j == 0:
                acc_b[...] = part
            else:
                acc_b[...] += part
    norm_back(tok_t, gain[0], acc_b, acc_a, acc_a, None, sum_a, sum_b, None)
    vec[:, 0:1] = lane_sum(sum_a[...])
    vec[:, 3:4] = lane_sum(sum_b[...])
    gtok[...] = acc_a[...].T
    small[...] = jnp.zeros_like(small)
    small[0:16, :] = vec[...].T[0:16]
    for g in range(groups):
        small[16 + 8 * g : 24 + 8 * g, :hw] = bvec[g].T[0:8]
        small[32 + 8 * g : 40 + 8 * g, :ublk] = ubias[g].T[0:8]


def compute(hd, lw, head_on, ints, tok, cot, enc, ws, os_, wc, oc, wu, wd, cols, bcols, bup):
    tokens, width = tok.shape
    groups, _, _, hw = ws.shape
    units = wu.shape[2]
    sents = (ints.shape[0] - 1) // 2
    slots = tokens // sents
    heads = groups * hw // hd
    pad = -(-3 * hw // 128) * 128
    first = 3 * hw % 128
    shape = jax.ShapeDtypeStruct
    tall = pltpu.VMEM((width, tokens), F32)
    low = pltpu.VMEM((width, tokens), BF16)
    feat = pltpu.VMEM((groups * hw, tokens), BF16)
    attn = pltpu.VMEM((groups, first + hw, tokens), BF16)
    prob = pltpu.VMEM((heads * sents, slots, slots), BF16)
    sums = pltpu.VMEM((width, 128), F32)
    vm, sm = pl.BlockSpec(memory_space=pltpu.VMEM), pl.BlockSpec(memory_space=pltpu.SMEM)
    return pl.pallas_call(
        functools.partial(compute_kernel, hd),
        out_shape=(
            shape((tokens, width), F32),
            shape((tokens, width), F32),
            shape((tokens, width), BF16),
            shape((groups, width, 4 * hw), BF16),
            shape((groups, width, 4 * hw), BF16),
            shape((groups, width, units), BF16),
            shape((groups, width, units), BF16),
            shape((48, width), F32),
        ),
        in_specs=[sm] * 3 + [vm] * 7 + [ANY] * 2 + [vm] * 3,
        out_specs=(vm,) * 5 + (ANY,) * 2 + (vm,),
        scratch_shapes=[low] + [tall] * 4 + [low] * 6 + [feat] * 6 + [attn] * 2 + [prob] * 2
        + [pltpu.VMEM((groups, pad, tokens), BF16), feat] + [sums] * 4
        + [pltpu.VMEM((groups, hw, 128), F32), pltpu.VMEM((groups, bup.shape[1], 128), F32)]
        + [pltpu.VMEM((2, width, bup.shape[1]), BF16), pltpu.VMEM((2, bup.shape[1], width), BF16)]
        + [pltpu.VMEM((2, width, bup.shape[1]), BF16)] * 2
        + [pltpu.SemaphoreType.DMA((2, 2))] * 2,
        compiler_params=pltpu.CompilerParams(vmem_limit_bytes=63 << 20),
    )(lw, head_on, ints, tok, cot, enc, ws, os_, wc, oc, wu, wd, cols, bcols, bup)


def place():
    return tuple(lax.axis_index(name) for name in ("row", "dp", "mp"))


def send(src, dst, send_sem, recv_sem, peer):
    copy = pltpu.make_async_remote_copy(
        src_ref=src, dst_ref=dst, send_sem=send_sem, recv_sem=recv_sem,
        device_id=peer, device_id_type=MESH,
    )
    copy.start()
    return copy


def greet(peers):
    barrier = pltpu.get_barrier_semaphore()
    for peer in peers:
        pl.semaphore_signal(barrier, inc=1, device_id=peer, device_id_type=MESH)
    pl.semaphore_wait(barrier, len(peers))


def gather_kernel(n_row, n_in, *refs):
    encoder, halves = refs[0], refs[1 : 1 + n_in]
    land, wholes = refs[1 + n_in], refs[2 + n_in : 2 + 2 * n_in]
    send_sem, recv_sem, local_sem = refs[2 + 2 * n_in :]
    r, d, c = place()
    rows = land.shape[1]
    partner = (r, d, 1 - c)
    others = [(lax.rem(r + i, n_row), d, c) for i in range(1, n_row)]
    greet([partner] + others)
    copies = []
    for i, peer in enumerate(others):
        start = pl.multiple_of(peer[0] * (2 * rows) + c * rows, rows)
        copies.append(
            send(encoder.at[pl.ds(start, rows)], land.at[r], send_sem.at[i], recv_sem.at[i], peer)
        )
    for i, (half, whole) in enumerate(zip(halves, wholes)):
        j = n_row - 1 + i
        copies.append(send(half, whole.at[c], send_sem.at[j], recv_sem.at[j], partner))
        own = pltpu.make_async_copy(half, whole.at[c], local_sem.at[i])
        own.start()
        copies.append(own)
    start = pl.multiple_of(r * (2 * rows) + c * rows, rows)
    own = pltpu.make_async_copy(encoder.at[pl.ds(start, rows)], land.at[r], local_sem.at[n_in])
    own.start()
    copies.append(own)
    for copy in copies:
        copy.wait()


def gather(n_row, rows, encoder, halves):
    shape = jax.ShapeDtypeStruct
    out = [shape((n_row, rows, encoder.shape[1]), encoder.dtype)]
    out += [shape((2,) + half.shape, half.dtype) for half in halves]
    sems = n_row - 1 + len(halves)
    return pl.pallas_call(
        functools.partial(gather_kernel, n_row, len(halves)),
        out_shape=tuple(out),
        in_specs=[ANY] * (1 + len(halves)),
        out_specs=(VMEM,) * len(out),
        scratch_shapes=[
            pltpu.SemaphoreType.DMA((sems,)),
            pltpu.SemaphoreType.DMA((sems,)),
            pltpu.SemaphoreType.DMA((len(halves) + 1,)),
        ],
        compiler_params=pltpu.CompilerParams(
            collective_id=0, has_side_effects=True, vmem_limit_bytes=40 << 20
        ),
    )(encoder, *halves)


def window(rows, share):
    wide = max(
        -(-(i + 1) * share // 16) * 16 - i * share // 16 * 16 for i in range(rows // share)
    )
    return wide, lambda i: pl.multiple_of(
        jnp.minimum(i * share // 16 * 16, rows - wide), 16
    )


def scatter_kernel(n_row, n_dp, n_part, *refs):
    grads, (small, gmem, block, gtok) = refs[:n_part], refs[n_part : n_part + 4]
    refs = refs[n_part + 4 :]
    shards, (small_out, land, block_in, gtok_in) = refs[:n_part], refs[n_part : n_part + 4]
    refs = refs[n_part + 4 :]
    held, came, came_dp, low, came_row = [refs[i * n_part : (i + 1) * n_part] for i in range(5)]
    refs = refs[5 * n_part :]
    small_mp, small_dp, small_row, s_one, r_one, s_grad, r_grad, s_small, r_small, s_mem, r_mem, local_sem = refs
    r, d, c = place()
    rows = held[0].shape[1]
    wide, start_of = window(rows, rows // n_dp)
    partner = (r, d, 1 - c)
    rings = [(r, lax.rem(d + i, n_dp), c) for i in range(1, n_dp)]
    lines = [(lax.rem(r + i, n_row), d, c) for i in range(1, n_row)]
    greet([partner] + rings + lines)
    late = []

    first = []
    for i in range(n_part):
        first.append(send(grads[i].at[1 - c], came[i], s_one.at[i], r_one.at[i], partner))
        own = pltpu.make_async_copy(grads[i].at[c], held[i], local_sem.at[i])
        own.start()
        first.append(own)
    small_copy = send(small, small_mp, s_small.at[0], r_small.at[0], partner)
    mem = []
    for i, peer in enumerate(lines):
        mem.append(send(gmem, land.at[r, c], s_mem.at[i], r_mem.at[i], peer))
    own = pltpu.make_async_copy(gmem, land.at[r, c], local_sem.at[n_part])
    own.start()
    late.append(own)
    k = n_row - 1
    late.append(send(gmem, land.at[r, c], s_mem.at[k], r_mem.at[k], partner))
    late.append(send(block, block_in, s_one.at[n_part], r_one.at[n_part], partner))
    late.append(send(gtok, gtok_in, s_one.at[n_part + 1], r_one.at[n_part + 1], partner))

    over_dp = []
    for i in range(n_part):
        first[2 * i].wait()
        first[2 * i + 1].wait()

        @pl.loop(0, n_row)
        def _(z, i=i):
            @pl.loop(0, rows // 16)
            def _(j):
                at = lanes(j, 16)
                held[i][z, at] = (
                    held[i][z, at].astype(F32) + came[i][z, at].astype(F32)
                ).astype(BF16)

        over_dp.append([
            send(
                held[i].at[:, pl.ds(start_of(peer[1]), wide)], came_dp[i].at[j],
                s_grad.at[i, j], r_grad.at[i, j], peer,
            )
            for j, peer in enumerate(rings)
        ])
    small_copy.wait()
    small_dp[d] = small[...] + small_mp[...]
    small_over = [
        send(small_dp.at[d], small_dp.at[d], s_small.at[1 + j], r_small.at[1 + j], peer)
        for j, peer in enumerate(rings)
    ]

    over_row = []
    for i in range(n_part):
        for copy in over_dp[i]:
            copy.wait()

        @pl.loop(0, n_row)
        def _(z, i=i):
            total = held[i][z, pl.ds(start_of(d), wide)].astype(F32)
            for j in range(n_dp - 1):
                total += came_dp[i][j, z].astype(F32)
            low[i][z] = total.astype(BF16)

            @pl.when(z == r)
            def _():
                shards[i][...] = total

        over_row.append([
            send(
                low[i].at[peer[0]], came_row[i].at[j],
                s_grad.at[i, n_dp - 1 + j], r_grad.at[i, n_dp - 1 + j], peer,
            )
            for j, peer in enumerate(lines)
        ])
    for copy in small_over:
        copy.wait()
    total = small_dp[0]
    for j in range(1, n_dp):
        total += small_dp[j]
    small_row[r] = total
    small_over = [
        send(small_row.at[r], small_row.at[r], s_small.at[n_dp + j], r_small.at[n_dp + j], peer)
        for j, peer in enumerate(lines)
    ]

    for i in range(n_row - 1):
        mem[i].wait()
        origin = lax.rem(r + n_row - 1 - i, n_row)
        late.append(
            send(
                land.at[origin, c], land.at[origin, c], s_mem.at[n_row + i], r_mem.at[n_row + i], partner
            )
        )
    for i in range(n_part):
        for copy in over_row[i]:
            copy.wait()
        for j in range(n_row - 1):
            shards[i][...] += came_row[i][j].astype(F32)
    for copy in small_over:
        copy.wait()
    total = small_row[0]
    for j in range(1, n_row):
        total += small_row[j]
    small_out[...] = total
    for copy in late:
        copy.wait()


def scatter(n_row, n_dp, grads, small, gmem, block, gtok):
    shape = jax.ShapeDtypeStruct
    n = len(grads)
    tokens, width = gmem.shape
    rows = width // n_row
    wide, _ = window(rows, rows // n_dp)
    grads = [g.reshape(2, n_row, rows, g.shape[2]) for g in grads]
    full = [pltpu.VMEM(g.shape[1:], BF16) for g in grads]
    rings = [pltpu.VMEM((n_dp - 1, n_row, wide, g.shape[3]), BF16) for g in grads]
    lows = [pltpu.VMEM((n_row, wide, g.shape[3]), BF16) for g in grads]
    lines = [pltpu.VMEM((n_row - 1, wide, g.shape[3]), BF16) for g in grads]
    dma = pltpu.SemaphoreType.DMA
    return pl.pallas_call(
        functools.partial(scatter_kernel, n_row, n_dp, n),
        out_shape=tuple(shape((wide, g.shape[3]), F32) for g in grads)
        + (
            shape(small.shape, F32),
            shape((n_row, 2, tokens, width), BF16),
            shape(block.shape, F32),
            shape(gtok.shape, F32),
        ),
        in_specs=[ANY] * n + [VMEM] * 2 + [ANY] * 2,
        out_specs=(VMEM,) * (n + 1) + (ANY,) * 3,
        scratch_shapes=full + full + rings + lows + lines
        + [
            pltpu.VMEM(small.shape, F32),
            pltpu.VMEM((n_dp,) + small.shape, F32),
            pltpu.VMEM((n_row,) + small.shape, F32),
            dma((n + 2,)), dma((n + 2,)),
            dma((n, n_dp + n_row - 2)), dma((n, n_dp + n_row - 2)),
            dma((n_dp + n_row - 1,)), dma((n_dp + n_row - 1,)),
            dma((2 * n_row - 1,)), dma((2 * n_row - 1,)),
            dma((n + 1,)),
        ],
        compiler_params=pltpu.CompilerParams(
            collective_id=1, has_side_effects=True, vmem_limit_bytes=60 << 20
        ),
    )(*grads, small, gmem, block, gtok)


def per_device(
    tokens, encoder, layer_pick, piece_heads, piece_ffn, tgt_len, src_len, norm_gain, norm_shift,
    out_bias, w_self, o_self, b_self, w_cross, o_cross, b_cross, w_up, b_up, w_down, cotangent,
):
    n_row, n_dp = lax.axis_size("row"), lax.axis_size("dp")
    r, d, c = place()
    width = tokens.shape[1]
    half = tokens.shape[0] // 2
    sents = tgt_len.shape[0] // 2
    units, hw = w_up.shape[1], w_self.shape[2]
    chosen = lax.dynamic_index_in_dim(layer_pick, r, 0, keepdims=False).astype(F32)
    layer_weight = chosen / jnp.sum(chosen)
    head_limit = lax.dynamic_index_in_dim(piece_heads, r, 0, keepdims=False)
    unit_limit = lax.dynamic_index_in_dim(piece_ffn, r, 0, keepdims=True)
    head_on = (jnp.arange(2 * hw // HD) < head_limit).astype(F32)
    lengths = [lax.dynamic_slice_in_dim(v, c * sents, sents) for v in (tgt_len, src_len)]
    ints = jnp.concatenate([unit_limit] + lengths)
    cols = jnp.concatenate([norm_gain, norm_shift, out_bias]).T
    bcols = jnp.concatenate([b_self, b_cross]).T
    ublk = 256
    bup = jnp.pad(b_up.reshape(-1, ublk).T, ((0, 0), (0, 128 - units // ublk)))
    own = lambda v: lax.dynamic_slice_in_dim(v, c * half, half)
    encoder = encoder.reshape(-1, width)

    land, ws, os_, wc, oc, wu, wd, bcols, bup = gather(
        n_row, half, encoder, (w_self, o_self, w_cross, o_cross, w_up, w_down, bcols, bup)
    )
    block, gtok, gmem, *grads, small = compute(
        HD, layer_weight, head_on, ints, own(tokens), own(cotangent), land,
        ws, os_, wc, oc, wu, wd, cols, bcols, bup,
    )
    rows = width // n_row
    share = rows // n_dp

    def both(mine, other):
        return jnp.where(
            c == 0, jnp.concatenate([mine, other]), jnp.concatenate([other, mine])
        )

    if n_dp <= 8:
        *shards, small, glad, block_in, gtok_in = scatter(
            n_row, n_dp, grads, small, gmem, block, gtok
        )
        _, start_of = window(rows, share)
        shards = [
            lax.dynamic_slice_in_dim(v, share * d - start_of(d), share) for v in shards
        ]
        block, gtok = both(block, block_in), both(gtok, gtok_in)
    else:
        shards = [
            lax.psum_scatter(
                lax.dynamic_index_in_dim(lax.psum(v.astype(F32), "mp"), c, 0, keepdims=False),
                ("row", "dp"), scatter_dimension=0, tiled=True,
            )
            for v in grads
        ]
        small = lax.psum(small, ("row", "dp", "mp"))
        glad = lax.all_gather(gmem, ("row", "mp")).reshape(n_row, 2, half, width)
        block, gtok = [lax.all_gather(v, "mp", tiled=True) for v in (block, gtok)]

    mine = lax.dynamic_index_in_dim(layer_pick, r, 1, keepdims=False).astype(F32)
    totals = jnp.sum(layer_pick.astype(F32), axis=1)
    grad_encoder = (mine / totals)[:, None, None, None] * glad.astype(F32)
    at = (r * n_dp + d) * share
    norms = lax.dynamic_slice_in_dim(small[:9], at, share, axis=1)
    heads = lax.dynamic_slice_in_dim(small, 16 + 8 * c, 8)[:4, :hw]
    ups = lax.dynamic_slice_in_dim(small, 32 + 8 * c, 8)[: units // ublk, :ublk]
    cut = lambda v, i: v[:, i * hw : (i + 1) * hw]
    w_s, w_x, w_u, w_d = shards
    return (
        block,
        gtok,
        grad_encoder.reshape(1, -1, width),
        norms[0:3],
        norms[3:6],
        norms[6:9],
        jnp.stack([cut(w_s, 0), cut(w_s, 1), cut(w_s, 2)]),
        cut(w_s, 3).T,
        heads[0:2],
        jnp.stack([cut(w_x, 2), cut(w_x, 0), cut(w_x, 1)]),
        cut(w_x, 3).T,
        heads[2:4],
        w_u,
        ups.reshape(units),
        w_d.T,
    )


def solution(mesh):
    return jax.shard_map(
        per_device,
        mesh=mesh,
        in_specs=(
            P(("row", "dp"), None),
            P("row", "dp", None),
            P(),
            P(),
            P(),
            P(("row", "dp")),
            P(("row", "dp")),
            P(),
            P(),
            P(),
            P(None, None, "mp"),
            P("mp", None),
            P(None, "mp"),
            P(None, None, "mp"),
            P("mp", None),
            P(None, "mp"),
            P(None, "mp"),
            P("mp"),
            P("mp", None),
            P(("row", "dp"), None),
        ),
        out_specs=(
            P(("row", "dp"), None),
            P(("row", "dp"), None),
            P("row", "dp", None),
            P(None, ("row", "dp")),
            P(None, ("row", "dp")),
            P(None, ("row", "dp")),
            P(None, ("row", "dp"), "mp"),
            P("mp", ("row", "dp")),
            P(None, "mp"),
            P(None, ("row", "dp"), "mp"),
            P("mp", ("row", "dp")),
            P(None, "mp"),
            P(("row", "dp"), "mp"),
            P("mp"),
            P("mp", ("row", "dp")),
        ),
        check_vma=False,
    )
```

time: 1390 us -> 342 us (0.25)
  waiting for transfers between devices: 1000 us -> 0 us
  Pallas kernels: 0 us -> 292 us
  matrix products: 130 us -> 0 us
  blocking collectives: 75.7 us -> 0 us
  local copies, waits for them, and re-layouts: 93.3 us -> 30.4 us
  other arithmetic: 45.4 us -> 18.2 us
  between operations: 16.3 us -> 0.88 us
  starting transfers between devices: 14.4 us -> 0 us
    unnamed x13 -> x0, waiting for transfers between devices: 597 us -> none
    pallas_call x0 -> x3, Pallas kernels: none -> 292 us  [the longest x1 145 us: scatter(): pl.pallas_call(functools.partial(scatter_kernel, n_row, n_dp, n), out_sha...]
    reduce_scatter x2 -> x0, waiting for transfers between devices: 279 us -> none  [the longest x1 139 us: per_device(): lax.psum_scatter(grad_w_down, ('row', 'dp'), scatter_dimension=1, tiled=T...]
    dot_general x35 -> x0, matrix products: 130 us -> none  [the longest x2 17.5 us: attend_backward(): jnp.einsum('ghqk,gqhd->gkhd', grad_score, query_low, preferred_element_ty...]
    unnamed x1 -> x0, blocking collectives: 75.7 us -> none
    psum x5 -> x0, waiting for transfers between devices: 74.2 us -> none  [the longest x1 23.3 us: per_device(): lax.psum(jnp.dot(attn_one, o_self, preferred_element_type=jnp.float32), '...]
    all_to_all x2 -> x0, waiting for transfers between devices: 51.9 us -> none  [the longest x1 51.9 us: per_device(): lax.all_to_all(stacked, 'row', split_axis=0, concat_axis=0, tiled=True)]
    reduce_sum x21 -> x2, other arithmetic: 28.3 us -> 1.41 us  [the longest x1 1.29 us: per_device(): layer_weight = chosen / jnp.sum(chosen)]
  transfers between devices with their start and end apart: 12 -> 0, of which waited for: 11 -> 0; matrix products, arithmetic and copies ran while one was open for 9% -> 0% of each run, Pallas kernels for 0% -> 0%
where the time goes in v1:
time: 342 us
  Pallas kernels  292 us (85%)
  local copies, waits for them, and re-layouts  30.4 us (9%)
  other arithmetic  18.2 us (5%)
    pallas_call x1, Pallas kernels, scatter(): pl.pallas_call(functools.partial(scatter_kernel, n_row, n_dp, n), out_sha...  145 us
    pallas_call x1, Pallas kernels, compute(): pl.pallas_call(functools.partial(compute_kernel, hd), out_shape=(shape((t...  93 us
    pallas_call x1, Pallas kernels, gather(): pl.pallas_call(functools.partial(gather_kernel, n_row, len(halves)), out_...  54.1 us
    unnamed x50, local copies, waits for them, and re-layouts  14.4 us
    mul x1, other arithmetic, per_device(): grad_encoder = (mine / totals)[:, None, None, None] * glad.astype(F32)  7.6 us

profile of v1, /device:TPU:0, one launch (start us, length us, event | category | flops | bytes accessed | tf_op | source)
XLA Modules:
  0.0 341.7 jit_solution(520487748680497994)
XLA Ops:
  0.7 0.8 dynamic_slice.52
  1.5 0.7 dynamic_slice.53
  2.2 1.2 dynamic_slice.51
  3.5 1.2 pad_add_fusion.ints
  4.7 1.3 fusion.3
  6.0 1.8 divide_bitcast_fusion.lw
  7.8 2.5 constant_dynamic-slice_fusion.6
  10.3 0.6 dynamic_slice.50
  10.9 1.2 compare_convert_fusion.head_on
  12.1 0.9 copy.52.refs_1_
  13.0 2.5 copy.53.refs_3_
  15.6 0.0 copy-done.20
  15.6 0.1 copy.51
  15.8 0.1 copy.50
  15.9 0.0 copy-start.1
  15.9 1.5 copy-done.1
  17.5 1.5 copy-done.2
  19.0 1.0 copy-done.5
  20.0 1.0 copy-done.6
  21.0 54.1 %shard_map.307 = (bf16[4,512,640]{2,1,0:T(8,128)(2,1)S(1)}, bf16[2,3,640,320]{3,2,1,0:T(8,128)(2,1)}, bf16[2,320,640]{2,1,0:T(8,128)(2,1)S(1)}, bf16[2,3,640,320...) custom-call(bf16[4096,640]{1,0:T(8,128)(2,1)} %bitcast.32, ...), custom_call_target="tpu_custom_call" | custom-call | tf_op jit(solution)/shard_map/pallas_call | solution.py:415
  75.1 0.0 copy-start
  75.1 1.5 copy-done
  76.6 0.9 copy-done.3
  77.5 0.9 copy-done.4
  78.4 0.8 copy-done.7
  79.2 0.7 copy-done.8
  79.9 0.9 copy.54
  80.8 93.0 %shard_map.308 = (f32[512,640]{1,0:T(8,128)}, f32[512,640]{1,0:T(8,128)}, bf16[512,640]{1,0:T(8,128)(2,1)}, bf16[2,640,1280]{2,1,0:T(8,128)(2,1)}, bf16[2,640,12...) custom-call(f32[4]{0:T(128)} %divide_bitcast_fusion.lw, ...), custom_call_target="tpu_custom_call" | custom-call | tf_op jit(solution)/shard_map/pallas_call | solution.py:337
  173.8 0.0 copy-start.16
  173.8 145.2 %shard_map.309 = (f32[48,1280]{1,0:T(8,128)}, f32[48,1280]{1,0:T(8,128)}, f32[48,1536]{1,0:T(8,128)}, f32[48,1536]{1,0:T(8,128)}, f32[48,640]{1,0:T(8,128)}, /*i...) custom-call(bf16[2,4,160,1280]{3,2,1,0:T(8,128)(2,1)} %bitcast.35, ...), custom_call_target="tpu_custom_call" | custom-call | tf_op jit(solution)/shard_map/pallas_call | solution.py:572
  319.0 1.7 dynamic-slice_bitcast_fusion.1
  320.8 0.7 pad_maximum_fusion.1
  321.4 1.7 dynamic-slice_bitcast_fusion.5
  323.2 0.7 pad_maximum_fusion
  323.9 0.2 fusion.1
  324.0 0.1 convert_reduce_fusion
  324.2 7.6 %convert_multiply_fusion = f32[4,2,512,640]{3,2,1,0:T(8,128)} fusion(bf16[4,2,512,640]{3,2,1,0:T(8,128)(2,1)} %get-tuple-element.59, f32[4]{0:T(128)S(1)} %div.29), kind=kLoop, calls=%fused_computation | loop fusion | flops 5242880 | bytes 15728656 | tf_op jit(solution)/shard_map/mul | solution.py:662
  331.8 1.7 maximum_select_fusion.1
  333.5 0.1 copy-done.9
  333.6 0.8 copy-done.11
  334.5 1.7 maximum_select_fusion
  336.1 0.7 constant_dynamic-slice_fusion.3
  336.8 0.7 dynamic-slice_bitcast_fusion
  337.6 0.8 slice.48
  338.3 0.7 fusion.4
  339.0 0.7 constant_dynamic-slice_fusion.2
  339.7 0.6 reshape.73
  340.3 1.4 constant_dynamic-slice_fusion.4
  (38 shorter events, 0.1 us)
Async XLA Ops:
  0.6 9.7 %copy-start.23 = (s32[4]{0:T(128)S(1)}, s32[4]{0:T(128)}, u32[]{:S(2)}) copy-start(s32[4]{0:T(128)} %param.23) | copy-start | bytes 52
  0.7 11.4 %copy-start.13 = (bf16[3,640,320]{1,2,0:T(8,128)(2,1)S(1)}, bf16[3,640,320]{1,2,0:T(8,128)(2,1)}, u32[]{:S(2)}) copy-start(bf16[3,640,320]{1,2,0:T(8,128)(2,1)} %param.30) | copy-start | bytes 3686404
  12.1 3.5 %copy-start.20 = (f32[1536]{0:T(1024)S(1)}, f32[1536]{0:T(1024)}, u32[]{:S(2)}) copy-start(f32[1536]{0:T(1024)} %param.37) | copy-start | bytes 18436
  12.1 3.7 %copy-start.21 = (f32[2,320]{1,0:T(2,128)S(1)}, f32[2,320]{1,0:T(2,128)}, u32[]{:S(2)}) copy-start(f32[2,320]{1,0:T(2,128)} %param.35) | copy-start | bytes 7684
  12.1 3.7 %copy-start.22 = (f32[2,320]{1,0:T(2,128)S(1)}, f32[2,320]{1,0:T(2,128)}, u32[]{:S(2)}) copy-start(f32[2,320]{1,0:T(2,128)} %param.32) | copy-start | bytes 7684
  15.9 1.6 copy-start.1
  17.5 1.5 copy-start.2
  19.0 1.0 copy-start.5
  20.0 1.0 copy-start.6
  21.0 58.8 %copy-start.17 = (f32[3,640]{1,0:T(4,128)S(1)}, f32[3,640]{1,0:T(4,128)}, u32[]{:S(2)}) copy-start(f32[3,640]{1,0:T(4,128)} %param.29) | copy-start | bytes 23044
  21.0 58.8 %copy-start.18 = (f32[3,640]{1,0:T(4,128)S(1)}, f32[3,640]{1,0:T(4,128)}, u32[]{:S(2)}) copy-start(f32[3,640]{1,0:T(4,128)} %param.28) | copy-start | bytes 23044
  21.0 58.8 %copy-start.19 = (f32[3,640]{1,0:T(4,128)S(1)}, f32[3,640]{1,0:T(4,128)}, u32[]{:S(2)}) copy-start(f32[3,640]{1,0:T(4,128)} %param.27) | copy-start | bytes 23044
  75.1 1.5 copy-start
  76.6 0.9 copy-start.3
  77.5 0.9 copy-start.4
  78.4 0.8 copy-start.7
  79.2 0.7 copy-start.8
  173.8 150.1 %copy-start.16 = (s32[4,4]{1,0:T(4,128)S(1)}, s32[4,4]{1,0:T(4,128)}, u32[]{:S(2)}) copy-start(s32[4,4]{1,0:T(4,128)} %param.22) | copy-start | bytes 196
  324.2 7.6 %copy-start.10 = (f32[512,640]{1,0:T(8,128)S(1)}, f32[512,640]{1,0:T(8,128)}, u32[]{:S(2)}) copy-start(f32[512,640]{1,0:T(8,128)} %get-tuple-element.56.refs_7_) | copy-start | bytes 3932164
  324.2 7.6 %copy-start.12 = (f32[512,640]{1,0:T(8,128)S(1)}, f32[512,640]{1,0:T(8,128)}, u32[]{:S(2)}) copy-start(f32[512,640]{1,0:T(8,128)} %get-tuple-element.58) | copy-start | bytes 3932164
  331.8 1.8 copy-start.9
  331.8 2.7 copy-start.11
  334.5 1.7 copy-start.15
  334.5 2.4 copy-start.14

commit v2 on v0

v2 whole, which is shorter than its diff:
```python
import functools
import types
import jax
import jax.numpy as jnp
from jax import lax
from jax.experimental import pallas as pl
from jax.experimental.pallas import tpu as pltpu
from jax.sharding import PartitionSpec as P

HD = 80
EPSILON = 1e-05
MASKED = -1e30
F32, BF16 = jnp.float32, jnp.bfloat16
MESH = pl.DeviceIdType.MESH
ANY = pl.BlockSpec(memory_space=pl.ANY)
VMEM = pl.BlockSpec(memory_space=pltpu.VMEM)


def nn(a, b):
    return lax.dot_general(a, b, (((1,), (0,)), ((), ())), preferred_element_type=F32)


def nt(a, b):
    return lax.dot_general(a, b, (((1,), (1,)), ((), ())), preferred_element_type=F32)


def tn(a, b):
    return lax.dot_general(a, b, (((0,), (0,)), ((), ())), preferred_element_type=F32)


def lanes(i, n):
    return pl.ds(pl.multiple_of(i * n, n), n)


def layer_norm(v_ref, x_ref, gain, shift, begin, end):
    @pl.loop(begin // 128, end // 128)
    def _(i):
        v = v_ref[:, lanes(i, 128)].astype(F32)
        c = v - jnp.mean(v, axis=0, keepdims=True)
        r = lax.rsqrt(jnp.mean(c * c, axis=0, keepdims=True) + EPSILON)
        x_ref[:, lanes(i, 128)] = (c * r * gain + shift).astype(BF16)


def norm_back(v_ref, gain, up_ref, base_ref, out_ref, low_ref, sums, begin, end):
    gain_sum, shift_sum, bias_sum = sums
    if begin == 0:
        for ref in sums:
            ref[...] = jnp.zeros_like(ref)

    @pl.loop(begin // 128, end // 128)
    def _(i):
        at = lanes(i, 128)
        v = v_ref[:, at].astype(F32)
        c = v - jnp.mean(v, axis=0, keepdims=True)
        r = lax.rsqrt(jnp.mean(c * c, axis=0, keepdims=True) + EPSILON)
        xhat = c * r
        e = up_ref[:, at]
        gain_sum[...] += e * xhat
        shift_sum[...] += e
        eg = e * gain
        m1 = jnp.mean(eg, axis=0, keepdims=True)
        m2 = jnp.mean(eg * xhat, axis=0, keepdims=True)
        out = base_ref[:, at].astype(F32) + r * (eg - m1 - xhat * m2)
        out_ref[:, at] = out
        low = out.astype(BF16)
        low_ref[:, at] = low
        bias_sum[...] += low.astype(F32)


def attend(q_ref, k_ref, v_ref, out_ref, prob_ref, masks, head_on, hd, per, sents):
    groups, slots = out_ref.shape[0], q_ref.shape[1] // sents
    first = out_ref.shape[1] - per * hd
    for g in range(groups):

        @pl.loop(0, per)
        def _(h, g=g):
            rows = pl.ds(pl.multiple_of((g * per + h) * hd, 16), hd)
            to = pl.ds(pl.multiple_of(first + h * hd, 16), hd)
            for s, mask in masks.items():
                at = slice(s * slots, (s + 1) * slots)
                scores = tn(k_ref[rows, at], q_ref[rows, at]) * hd ** (-0.5)
                scores = jnp.where(mask, scores, MASKED)
                e = jnp.exp(scores - jnp.max(scores, axis=0, keepdims=True))
                total = jnp.sum(e, axis=0, keepdims=True)
                p = (e * (1.0 / total)).astype(BF16)
                prob_ref[(g * per + h) * sents + s] = p
                mixed = nn(v_ref[rows, at], p) * head_on(g, h)
                out_ref[g, to, at] = mixed.astype(BF16)


def attend_back(q_ref, k_ref, v_ref, e_ref, prob_ref, d_ref, at_rows, hd, per, sents, some):
    groups, slots = d_ref.shape[0], q_ref.shape[1] // sents
    for g in range(groups):

        @pl.loop(0, per)
        def _(h, g=g):
            rows = pl.ds(pl.multiple_of((g * per + h) * hd, 16), hd)
            dq_at, dk_at, dv_at = [
                pl.ds(pl.multiple_of(first + h * hd, 16), hd) for first in at_rows
            ]
            for s in some:
                at = slice(s * slots, (s + 1) * slots)
                e, p = e_ref[rows, at], prob_ref[(g * per + h) * sents + s]
                d_ref[g, dv_at, at] = nt(e, p).astype(BF16)
                dp = tn(v_ref[rows, at], e)
                pf = p.astype(F32)
                delta = jnp.sum(pf * dp, axis=0, keepdims=True)
                ds = (pf * (dp - delta) * hd ** (-0.5)).astype(BF16)
                d_ref[g, dq_at, at] = nn(k_ref[rows, at], ds).astype(BF16)
                d_ref[g, dk_at, at] = nt(q_ref[rows, at], ds).astype(BF16)


def lane_sum(values):
    return jnp.sum(values.astype(F32), axis=1, keepdims=True)


def place():
    return tuple(lax.axis_index(name) for name in ("row", "dp", "mp"))


def window(rows, share):
    wide = max(
        -(-(i + 1) * share // 16) * 16 - i * share // 16 * 16 for i in range(rows // share)
    )
    return wide, lambda i: pl.multiple_of(
        jnp.minimum(i * share // 16 * 16, rows - wide), 16
    )


def remote(src, dst, send_sem, recv_sem, peer):
    return pltpu.make_async_remote_copy(
        src_ref=src, dst_ref=dst, send_sem=send_sem, recv_sem=recv_sem,
        device_id=peer, device_id_type=MESH,
    )


def started(copy):
    copy.start()
    return copy


def layer_kernel(n_row, n_dp, names, *args):
    refs = dict(zip(names, args))
    ref = types.SimpleNamespace(**refs)
    layer_pick, piece_heads, piece_ffn, tgt_len, src_len = (ref.layer_pick, ref.piece_heads, ref.piece_ffn, ref.tgt_len, ref.src_len)
    tokens, cotangent, encoder = (ref.tokens, ref.cotangent, ref.encoder)
    ws, wc, os_, oc, wu_buf, wd_buf = (ref.ws, ref.wc, ref.os, ref.oc, ref.wu_buf, ref.wd_buf)
    tok_in, cot_in, enc, tout, tok_t, mid_t, late_t, acc_a, acc_b = (ref.tok_in, ref.cot_in, ref.enc, ref.tout, ref.tok_t, ref.mid_t, ref.late_t, ref.acc_a, ref.acc_b)
    x1, x2, x3, ct, mem_t, e_low, eh = (ref.x1, ref.x2, ref.x3, ref.ct, ref.mem_t, ref.e_low, ref.eh)
    q1, k1, v1, q2, k2, v2 = (ref.q1, ref.k1, ref.v1, ref.q2, ref.k2, ref.v2)
    attn1, attn2, prob1, prob2, grads = (ref.attn1, ref.attn2, ref.prob1, ref.prob2, ref.grads)
    sum_a, sum_b, sum_c, vec, bvec, ubias, colm, cols, bm, bcols, bups = (ref.sum_a, ref.sum_b, ref.sum_c, ref.vec, ref.bvec, ref.ubias, ref.colm, ref.cols, ref.bm, ref.bcols, ref.bups)
    out_s, out_x, out_u, out_d, abuf = (ref.out_s, ref.out_x, ref.out_u, ref.out_d, ref.abuf)
    local_sem, send_sem, recv_sem, fetch_sem, push_sem, land_sem = (ref.local_sem, ref.send_sem, ref.recv_sem, ref.fetch_sem, ref.push_sem, ref.land_sem)
    held, came = (ref.held_s, ref.held_x, ref.held_u, ref.held_d), (ref.came_s, ref.came_x, ref.came_u, ref.came_d)
    small, glad = (ref.small, ref.glad)
    spread = n_dp == 4

    width, tokens_here = tok_t.shape
    groups, _, hw, _ = ws.shape
    units, ublk, hd = ref.w_up.shape[1], bups.shape[1], HD
    blocks, per = units // ublk, hw // HD
    rows = width // n_row
    sents = tgt_len.shape[0] // 2
    slots = tokens_here // sents
    pad = -(-3 * hw // 128) * 128
    lead = 3 * hw // 128 * 128
    first = 3 * hw - lead
    r, d, c = place()
    partner = (r, d, 1 - c)
    rings = [(r, lax.rem(d + i, n_dp), c) for i in range(1, n_dp)] if spread else []
    lines = [(lax.rem(r + i, n_row), d, c) for i in range(1, n_row)]
    counts = {"local": 0, "link": 0}

    def fetch(src, dst):
        i = counts["local"]
        counts["local"] += 1
        return started(pltpu.make_async_copy(src, dst, local_sem.at[i]))

    def push(src, dst, peer):
        i = counts["link"]
        counts["link"] += 1
        return started(remote(src, dst, send_sem.at[i], recv_sem.at[i], peer))

    mine = pl.ds(pl.multiple_of(c * tokens_here, tokens_here), tokens_here)
    tok_copy = fetch(tokens.at[mine], tok_in)
    ws_copies = [fetch(ref.w_self, ws.at[0]), fetch(ref.o_self, os_.at[0])]
    bm[...] = jnp.zeros_like(bm)
    bm[0, 0:2, :hw] = ref.b_self[...]
    bm[0, 2:4, :hw] = ref.b_cross[...]
    bm[0, 8 : 8 + blocks, :ublk] = ref.b_up[...]
    colm[...] = jnp.zeros_like(colm)
    colm[0:3] = ref.norm_gain[...]
    colm[3:6] = ref.norm_shift[...]
    colm[6:9] = ref.out_bias[...]
    barrier = pltpu.get_barrier_semaphore()
    peers = [partner] + rings + lines
    for peer in peers:
        pl.semaphore_signal(barrier, inc=1, device_id=peer, device_id_type=MESH)
    pl.semaphore_wait(barrier, len(peers))
    ws_copies += [
        push(ref.w_self, ws.at[1], partner),
        push(bm.at[0], bm.at[1], partner),
        push(ref.o_self, os_.at[1], partner),
    ]
    def sentence(piece, i):
        start = (piece * 2 + c) * tokens_here + i * slots
        return encoder.at[pl.ds(pl.multiple_of(start, slots), slots)]

    columns = [slice(i * slots, (i + 1) * slots) for i in range(sents)]

    def send_sentence(i):
        at = columns[i]
        copies = [push(sentence(peer[0], i), enc.at[r, at], peer) for peer in lines]
        return copies + [fetch(sentence(r, i), enc.at[r, at])]

    enc_copies = [send_sentence(0)]
    wc_copies = [
        fetch(ref.w_cross, wc.at[0]),
        fetch(ref.o_cross, oc.at[0]),
        push(ref.w_cross, wc.at[1], partner),
        push(ref.o_cross, oc.at[1], partner),
    ]
    cot_copy = fetch(cotangent.at[mine], cot_in)
    ffn_copies = [
        push(ref.w_up, ref.up_in, partner),
        push(ref.w_down, ref.down_in, partner),
    ]

    cols[...] = colm[...].T
    gain, shift, obias = [[cols[:, j : j + 1] for j in range(3 * i, 3 * i + 3)] for i in range(3)]
    key_at = lax.broadcasted_iota(jnp.int32, (slots, slots), 0)
    query_at = lax.broadcasted_iota(jnp.int32, (slots, slots), 1)
    for zeroed in (attn1, attn2):
        zeroed[:, :first, :] = jnp.zeros((groups, first, tokens_here), BF16)
    grads[:, 3 * hw :, :] = jnp.zeros((groups, pad - 3 * hw, tokens_here), BF16)
    vec[...] = jnp.zeros_like(vec)
    bvec[...] = jnp.zeros_like(bvec)
    ubias[...] = jnp.zeros_like(ubias)
    heads_here, units_here = piece_heads[r], piece_ffn[r]
    group_at = [c, 1 - c]

    def head_on(g, h):
        return jnp.where(group_at[g] * per + h < heads_here, 1.0, 0.0)

    tok_copy.wait()
    tok_t[...] = tok_in[...].astype(F32).T.astype(BF16)
    layer_norm(tok_t, x1, gain[0], shift[0], 0, tokens_here)
    for copy in ws_copies:
        copy.wait()
    for g in range(groups):
        bcols[g] = bm[g, 0:8].T
        bups[g] = bm[g, 8:16, :ublk].T
    for g in range(groups):
        at = slice(g * hw, (g + 1) * hw)
        q1[at] = (nn(ws[g, 0], x1[...]) + bcols[g, :hw, 0:1]).astype(BF16)
        k1[at] = nn(ws[g, 1], x1[...]).astype(BF16)
        v1[at] = (nn(ws[g, 2], x1[...]) + bcols[g, :hw, 1:2]).astype(BF16)
    masks = {
        i: (key_at <= query_at) & (key_at < tgt_len[c * sents + i]) for i in range(sents)
    }
    attend(q1, k1, v1, attn1, prob1, masks, head_on, hd, per, sents)
    acc_a[...] = tn(os_[0], attn1[0, first:])
    for g in range(1, groups):
        acc_a[...] += tn(os_[g], attn1[g, first:])
    mid_t[...] = tok_t[...].astype(F32) + acc_a[...] + obias[0]
    layer_norm(mid_t, x2, gain[1], shift[1], 0, tokens_here)
    for copy in wc_copies:
        copy.wait()
    for g in range(groups):
        at = slice(g * hw, (g + 1) * hw)
        q2[at] = (nn(wc[g, 0], x2[...]) + bcols[g, :hw, 2:3]).astype(BF16)
    cot_copy.wait()
    ct[...] = cot_in[...].astype(F32).T.astype(BF16)

    picks = [
        jnp.full((1, width), layer_pick[r, i].astype(F32), F32) for i in range(layer_pick.shape[1])
    ]
    total = functools.reduce(jnp.add, picks)
    weights = [pick / total for pick in picks]
    def cross(i):
        at = columns[i]
        for copy in enc_copies[i]:
            copy.wait()
        if i + 1 < sents:
            enc_copies.append(send_sentence(i + 1))
        memory = weights[0] * enc[0, at].astype(F32)
        for j in range(1, n_row):
            memory += weights[j] * enc[j, at].astype(F32)
        mem_t[:, at] = memory.T.astype(BF16)
        for g in range(groups):
            to = slice(g * hw, (g + 1) * hw)
            k2[to, at] = nn(wc[g, 1], mem_t[:, at]).astype(BF16)
            v2[to, at] = (nn(wc[g, 2], mem_t[:, at]) + bcols[g, :hw, 3:4]).astype(BF16)
        masks = {i: key_at < src_len[c * sents + i]}
        attend(q2, k2, v2, attn2, prob2, masks, head_on, hd, per, sents)
        branch = tn(oc[0], attn2[0, first:, at])
        for g in range(1, groups):
            branch += tn(oc[g], attn2[g, first:, at])
        late_t[:, at] = mid_t[:, at] + branch + obias[1]
        layer_norm(late_t, x3, gain[2], shift[2], at.start, at.stop)

    def fetches(phase, i):
        slot, at = lax.rem(phase * blocks + i, 2), lanes(i, ublk)
        up, down = (ref.w_up, ref.w_down) if phase else (ref.up_in, ref.down_in)
        return [
            pltpu.make_async_copy(up.at[:, at], wu_buf.at[slot], fetch_sem.at[0, slot]),
            pltpu.make_async_copy(down.at[at, :], wd_buf.at[slot], fetch_sem.at[1, slot]),
        ]

    def pushes(i, k):
        at = lanes(i, ublk)
        return remote(
            (out_u, out_d)[k].at[:, :, at], came[2 + k].at[:, :, at],
            push_sem.at[k, i], land_sem.at[k, i], partner,
        )

    def feed_forward(n, ready):
        cols_at = columns[n]
        if n == 0:
            for copy in ready:
                copy.wait()
            for copy in fetches(0, 0):
                copy.start()
        acc_a[:, cols_at] = jnp.zeros((width, slots), F32)
        acc_b[:, cols_at] = jnp.zeros((width, slots), F32)
        for phase in range(2):
            g = 1 - phase
            sink_u, sink_d = (held[2], held[3]) if phase else (out_u, out_d)

            @pl.loop(0, blocks)
            def _(i, phase=phase, g=g, sink_u=sink_u, sink_d=sink_d):
                slot, at = lax.rem(phase * blocks + i, 2), lanes(i, ublk)

                @pl.when(i + 1 < blocks)
                def _():
                    for copy in fetches(phase, i + 1):
                        copy.start()

                if phase == 0 or n + 1 < sents:

                    @pl.when(i + 1 == blocks)
                    def _():
                        for copy in fetches(1 - phase, 0):
                            copy.start()

                for copy in fetches(phase, i):
                    copy.wait()
                up, down = wu_buf.at[slot], wd_buf.at[slot]
                here = lax.broadcasted_iota(jnp.int32, bups.shape[1:], 1) == i
                h = nn(up[...].T, x3[:, cols_at]) + lane_sum(jnp.where(here, bups[g], 0.0))
                unit = group_at[g] * units + i * ublk
                unit = unit + lax.broadcasted_iota(jnp.int32, (ublk, 1), 0)
                on = jnp.where(unit < units_here, 1.0, 0.0)
                inner = 0.7978845608028654 * (h + 0.044715 * (h * h * h))
                t = jnp.tanh(inner)
                cdf = 0.5 * (1.0 + t)
                slope = cdf + 0.5 * h * (1.0 - t * t) * (
                    0.7978845608028654 * (1.0 + 3 * 0.044715 * h * h)
                )
                act = (h * cdf * on).astype(BF16)
                acc_a[:, cols_at] += tn(down[...], act)
                dh = (nn(down[...], ct[:, cols_at]) * slope * on).astype(BF16)
                in_sums = lax.broadcasted_iota(jnp.int32, ubias.shape[1:], 1) == i
                ubias[g] += jnp.where(in_sums, lane_sum(dh), 0.0)
                acc_b[:, cols_at] += nn(up[...], dh)
                shape = (n_row, rows, ublk)
                grad_u = nt(x3[:, cols_at], dh).reshape(shape)
                grad_d = nt(ct[:, cols_at], act).reshape(shape)
                if n > 0:
                    grad_u += sink_u[:, :, at].astype(F32)
                    grad_d += sink_d[:, :, at].astype(F32)
                sink_u[:, :, at] = grad_u.astype(BF16)
                sink_d[:, :, at] = grad_d.astype(BF16)
                if phase == 0 and n + 1 == sents:
                    for k in range(2):
                        pushes(i, k).start()

        tout[cols_at] = (late_t[:, cols_at] + acc_a[:, cols_at] + obias[2]).T
        norm_back(
            late_t, gain[2], acc_b, ct, acc_a, e_low, (sum_a, sum_b, sum_c),
            cols_at.start, cols_at.stop,
        )

    late = []
    half = rows // 2
    wide, start_of = window(half, half // 2)
    up, across = lax.div(d, 2), lax.rem(d, 2)
    ours = half * up + start_of(across)
    pieces = {
        "u": (2, 0, units, True),
        "d": (3, 0, units, False),
        "x_a": (1, 0, 2 * hw, True),
        "x_b": (1, 2 * hw, 4 * hw, False),
        "s_a": (0, 0, 2 * hw, True),
        "s_b": (0, 2 * hw, 4 * hw, False),
    }

    def add_in(part, begin, end, landing, places, shard=None):
        size = landing.shape[1]
        at = pl.ds(begin, end - begin)
        loads = [
            pltpu.make_async_copy(
                landing.at[z], abuf.at[z % 2, pl.ds(0, size), pl.ds(0, end - begin)],
                fetch_sem.at[0, z % 2],
            )
            for z in range(n_row)
        ]
        loads[0].start()
        for z in range(n_row):
            if z + 1 < n_row:
                loads[z + 1].start()
            loads[z].wait()
            for to, source, count in places:

                @pl.loop(0, count // 16)
                def _(j, z=z, to=to, source=source):
                    held_at = pl.ds(pl.multiple_of(to + 16 * j, 16), 16)
                    from_at = pl.ds(pl.multiple_of(source + 16 * j, 16), 16)
                    total = held[part][z, held_at, at].astype(F32)
                    total += abuf[z % 2, from_at, pl.ds(0, end - begin)].astype(F32)
                    held[part][z, held_at, at] = total.astype(BF16)
                    if shard is not None:

                        @pl.when(r == z)
                        def _():
                            shard[from_at, at] = total

    def take(part, arrived):
        for copy in arrived:
            copy()
        add_in(part, 0, held[part].shape[2], came[part], [(0, 0, rows)])

    def first_ring(name):
        if not spread:
            return []
        part, begin, end, tall_first = pieces[name]
        landing, at = refs["ring_" + name], pl.ds(begin, end - begin)
        if tall_first:
            peer = (r, lax.rem(d + 2, 4), c)
            return [push(held[part].at[:, pl.ds(half * (1 - up), half), at], landing, peer)]
        peer = (r, d + 1 - 2 * across, c)
        return [
            push(
                held[part].at[:, pl.ds(half * i + start_of(1 - across), wide), at],
                landing.at[:, pl.ds(wide * i, wide)], peer,
            )
            for i in range(2)
        ]

    def second_ring(name, copies):
        if not spread:
            return []
        part, begin, end, tall_first = pieces[name]
        landing, at = refs["ring_" + name], pl.ds(begin, end - begin)
        for copy in copies:
            copy.wait()
        if tall_first:
            add_in(part, begin, end, landing, [(half * up, 0, half)])
            peer, gone = (r, d + 1 - 2 * across, c), half * up + start_of(1 - across)
        else:
            places = [(half * i + start_of(across), wide * i, wide) for i in range(2)]
            add_in(part, begin, end, landing, places)
            peer, gone = (r, lax.rem(d + 2, 4), c), half * (1 - up) + start_of(across)
        gone = pl.multiple_of(gone, 16)
        return [push(held[part].at[:, pl.ds(gone, wide), at], refs["turn_" + name], peer)]

    def to_lines(name, copies):
        if not spread:
            return []
        part, begin, end, _ = pieces[name]
        for copy in copies:
            copy.wait()
        shard, line = refs["shard_" + "sxud"[part]], refs["line_" + "sxud"[part]]
        at, here = pl.ds(begin, end - begin), pl.multiple_of(ours, 16)
        add_in(part, begin, end, refs["turn_" + name], [(here, 0, wide)], shard)
        return [
            push(held[part].at[peer[0], pl.ds(here, wide), at], line.at[j, :, at], peer)
            for j, peer in enumerate(lines)
        ]

    def sum_lines(part, copies):
        if spread:
            shard, line = refs["shard_" + "sxud"[part]], refs["line_" + "sxud"[part]]
            for copy in copies:
                copy.wait()
            for j in range(n_row - 1):
                shard[...] += line[j].astype(F32)

    def heads_back(weight, at):
        for g in range(groups):
            for h in range(per):
                to = slice(h * hd, (h + 1) * hd)
                eh[g * hw + h * hd : g * hw + (h + 1) * hd, at] = (
                    nn(weight[g, to], e_low[:, at]) * head_on(g, h)
                ).astype(BF16)

    def cross_back(i):
        at = columns[i]
        heads_back(oc, at)
        attend_back(q2, k2, v2, eh, prob2, grads, (2 * hw, 0, hw), hd, per, sents, [i])
        total = jnp.zeros((width, slots), F32)
        for g in range(groups):
            total += tn(wc[g, 1], grads[g, :hw, at]) + tn(wc[g, 2], grads[g, hw : 2 * hw, at])
        tok_in[at] = total.T.astype(BF16)
        late.append(fetch(tok_in.at[at], glad.at[r, c, at]))
        late.append(push(tok_in.at[at], glad.at[r, c, at], partner))
        return [push(tok_in.at[at], glad.at[r, c, at], peer) for peer in lines]

    mem_copies = []
    for i in range(sents):
        cross(i)
        feed_forward(i, ffn_copies)
        if i + 1 == sents:
            block_copies = [fetch(tout, ref.block), push(tout, ref.block_in, partner)]
            take(2, [pushes(j, 0).wait for j in range(blocks)])
            ring_u = first_ring("u")
            take(3, [pushes(j, 1).wait for j in range(blocks)])
            ring_d = first_ring("d")
        mem_copies.append(cross_back(i))
    vec[:, 8:9] = lane_sum(ct[...])
    vec[:, 2:3] = lane_sum(sum_a[...])
    vec[:, 5:6] = lane_sum(sum_b[...])
    vec[:, 7:8] = lane_sum(sum_c[...])

    def put(g, begin, value):
        sink = (held_now, out_now)[g]
        at = pl.ds(begin, value.shape[1])
        sink[:, :, at] = value.astype(BF16).reshape(n_row, rows, -1)

    def weight_grads(g, sources, attn):
        tail = nt(e_low[...], attn[g])
        begin = 0
        for source, end in sources:
            while begin < end:
                step = min(256, end - begin)
                value = nt(source[...], grads[g, begin : begin + step])
                if begin + step == pad:
                    keep = lead - begin
                    if keep:
                        put(g, begin, value[:, :keep])
                    put(g, lead, value[:, keep:] + tail[:, : pad - lead])
                else:
                    put(g, begin, value)
                begin += step
        put(g, pad, tail[:, pad - lead :])

    held_now, out_now = held[1], out_x
    for g in (1, 0):
        bvec[g, :hw, 2:3] = lane_sum(grads[g, 2 * hw : 3 * hw])
        bvec[g, :hw, 3:4] = lane_sum(grads[g, hw : 2 * hw])
        weight_grads(g, [(mem_t, 2 * hw), (x2, pad)], attn2)
        if g == 1:
            came_x = push(out_x, came[1], partner)
            acc_b[...] = tn(wc[g, 0], grads[g, 2 * hw : 3 * hw])
        else:
            acc_b[...] += tn(wc[g, 0], grads[g, 2 * hw : 3 * hw])
    norm_back(
        mid_t, gain[1], acc_b, acc_a, acc_a, e_low, (sum_a, sum_b, sum_c), 0, tokens_here
    )
    vec[:, 1:2] = lane_sum(sum_a[...])
    vec[:, 4:5] = lane_sum(sum_b[...])
    vec[:, 6:7] = lane_sum(sum_c[...])
    take(1, [came_x.wait])
    ring_x = [first_ring("x_a"), first_ring("x_b")]

    heads_back(os_, slice(0, tokens_here))
    attend_back(q1, k1, v1, eh, prob1, grads, (0, hw, 2 * hw), hd, per, sents, range(sents))
    ring_u = second_ring("u", ring_u)
    ring_d = second_ring("d", ring_d)
    held_now, out_now = held[0], out_s
    for g in (1, 0):
        bvec[g, :hw, 0:1] = lane_sum(grads[g, :hw])
        bvec[g, :hw, 1:2] = lane_sum(grads[g, 2 * hw : 3 * hw])
        weight_grads(g, [(x1, pad)], attn1)
        if g == 1:
            came_s = push(out_s, came[0], partner)
    for g in range(groups):
        for j in range(3):
            part = tn(ws[g, j], grads[g, j * hw : (j + 1) * hw])
            if g == 0 and j == 0:
                acc_b[...] = part
            else:
                acc_b[...] += part
    take(0, [came_s.wait])
    ring_s = [first_ring("s_a"), first_ring("s_b")]
    ring_x = [second_ring("x_a", ring_x[0]), second_ring("x_b", ring_x[1])]
    norm_back(
        tok_t, gain[0], acc_b, acc_a, acc_a, e_low, (sum_a, sum_b, sum_c), 0, tokens_here
    )
    vec[:, 0:1] = lane_sum(sum_a[...])
    vec[:, 3:4] = lane_sum(sum_b[...])
    for copy in block_copies:
        copy.wait()
    tout[...] = acc_a[...].T
    late += [fetch(tout, ref.gtok), push(tout, ref.gtok_in, partner)]

    small[...] = jnp.zeros_like(small)
    small[0:16, :] = vec[...].T[0:16]
    for g in range(groups):
        at = pl.multiple_of(16 + 8 * group_at[g], 8)
        small[pl.ds(at, 8), :hw] = bvec[g].T[0:8, :hw]
        small[pl.ds(at + 16, 8), :ublk] = ubias[g].T[0:8]
    if spread:
        small_mp, small_dp, small_row = (ref.small_mp, ref.small_dp, ref.small_row)
        push(small, small_mp, partner).wait()
        small_dp[d] = small[...] + small_mp[...]
        small_copies = [push(small_dp.at[d], small_dp.at[d], peer) for peer in rings]
        line_u = to_lines("u", ring_u)
        line_d = to_lines("d", ring_d)
        ring_s = [second_ring("s_a", ring_s[0]), second_ring("s_b", ring_s[1])]
        for copy in small_copies:
            copy.wait()
        total = small_dp[0]
        for j in range(1, n_dp):
            total += small_dp[j]
        small_row[r] = total
        small_copies = [push(small_row.at[r], small_row.at[r], peer) for peer in lines]
        line_x = to_lines("x_a", ring_x[0]) + to_lines("x_b", ring_x[1])
    for at, copies in zip(columns, mem_copies):
        for i, copy in enumerate(copies):
            copy.wait()
            came_at = glad.at[lax.rem(r + n_row - 1 - i, n_row), c, at]
            late.append(push(came_at, came_at, partner))
    if spread:
        line_s = to_lines("s_a", ring_s[0]) + to_lines("s_b", ring_s[1])
        sum_lines(2, line_u)
        sum_lines(3, line_d)
        sum_lines(1, line_x)
        for copy in small_copies:
            copy.wait()
        total = small_row[0]
        for j in range(1, n_row):
            total += small_row[j]
        small[...] = total
        sum_lines(0, line_s)
    for copy in late:
        copy.wait()


def layer(n_row, n_dp, scalars, vectors, arrays):
    shape = jax.ShapeDtypeStruct
    encoder, w_self, w_up = arrays["encoder"], arrays["w_self"], arrays["w_up"]
    width, tokens = encoder.shape[1], arrays["tokens"].shape[0] // 2
    hw, units = w_self.shape[1], w_up.shape[1]
    blocks, ublk = vectors["b_up"].shape
    sents = scalars["tgt_len"].shape[0] // 2
    slots, heads = tokens // sents, 2 * hw // HD
    pad, first = -(-3 * hw // 128) * 128, 3 * hw % 128
    rows = width // n_row
    spread = n_dp == 4
    wide, _ = window(rows // 2, rows // 4)
    sizes = {"s": 4 * hw, "x": 4 * hw, "u": units, "d": units}
    outs = {
        "block": ((tokens, width), F32, ANY),
        "block_in": ((tokens, width), F32, ANY),
        "gtok": ((tokens, width), F32, ANY),
        "gtok_in": ((tokens, width), F32, ANY),
        "glad": ((n_row, 2, tokens, width), BF16, ANY),
        "small": ((48, width), F32, VMEM),
        "up_in": (w_up.shape, BF16, ANY),
        "down_in": (arrays["w_down"].shape, BF16, ANY),
    }
    scratch = {}
    for name, size in sizes.items():
        outs["came_" + name] = ((n_row, rows, size), BF16, ANY)
        if spread:
            for piece in (name,) if name in "ud" else (name + "_a", name + "_b"):
                tall_first = piece == "u" or piece[-1] == "a"
                cols_of = size if name in "ud" else size // 2
                landing = rows // 2 if tall_first else 2 * wide
                outs["ring_" + piece] = ((n_row, landing, cols_of), BF16, ANY)
                outs["turn_" + piece] = ((n_row, wide, cols_of), BF16, ANY)
            outs["shard_" + name] = ((wide, size), F32, VMEM)
            scratch["held_" + name] = pltpu.VMEM((n_row, rows, size), BF16)
            scratch["line_" + name] = pltpu.VMEM((n_row - 1, wide, size), BF16)
        else:
            outs["held_" + name] = ((n_row, rows, size), BF16, VMEM)
    tall, low = pltpu.VMEM((width, tokens), F32), pltpu.VMEM((width, tokens), BF16)
    flat = pltpu.VMEM((tokens, width), BF16)
    scratch["ws"] = scratch["wc"] = pltpu.VMEM((2,) + w_self.shape, BF16)
    scratch["os"] = scratch["oc"] = pltpu.VMEM((2, hw, width), BF16)
    scratch["wu_buf"] = pltpu.VMEM((2, width, ublk), BF16)
    scratch["wd_buf"] = pltpu.VMEM((2, ublk, width), BF16)
    scratch["out_u"] = scratch["out_d"] = pltpu.VMEM((n_row, rows, units), BF16)
    scratch["out_s"] = scratch["out_x"] = pltpu.VMEM((n_row, rows, 4 * hw), BF16)
    scratch["abuf"] = pltpu.VMEM((2, rows, max(sizes.values())), BF16)
    scratch["tok_in"] = scratch["cot_in"] = flat
    scratch["enc"] = pltpu.VMEM((n_row, tokens, width), BF16)
    scratch["tout"] = pltpu.VMEM((tokens, width), F32)
    for name in ("mid_t", "late_t", "acc_a", "acc_b"):
        scratch[name] = tall
    for name in ("tok_t", "x1", "x2", "x3", "ct", "mem_t", "e_low"):
        scratch[name] = low
    for name in ("q1", "k1", "v1", "q2", "k2", "v2", "eh"):
        scratch[name] = pltpu.VMEM((2 * hw, tokens), BF16)
    for name in ("attn1", "attn2"):
        scratch[name] = pltpu.VMEM((2, first + hw, tokens), BF16)
    for name in ("prob1", "prob2"):
        scratch[name] = pltpu.VMEM((heads * sents, slots, slots), BF16)
    scratch["grads"] = pltpu.VMEM((2, pad, tokens), BF16)
    for name in ("sum_a", "sum_b", "sum_c", "vec", "cols"):
        scratch[name] = pltpu.VMEM((width, 128), F32)
    scratch["colm"] = pltpu.VMEM((128, width), F32)
    scratch["bm"] = pltpu.VMEM((2, 16, width), F32)
    scratch["bvec"] = pltpu.VMEM((2, -(-hw // 128) * 128, 128), F32)
    scratch["bcols"] = pltpu.VMEM((2, width, 8), F32)
    scratch["ubias"] = pltpu.VMEM((2, ublk, 128), F32)
    scratch["bups"] = pltpu.VMEM((2, ublk, 8), F32)
    if spread:
        scratch["small_mp"] = pltpu.VMEM((48, width), F32)
        scratch["small_dp"] = pltpu.VMEM((n_dp, 48, width), F32)
        scratch["small_row"] = pltpu.VMEM((n_row, 48, width), F32)
    dma = pltpu.SemaphoreType.DMA
    scratch["local_sem"] = dma((16,))
    scratch["send_sem"] = scratch["recv_sem"] = dma((80,))
    scratch["fetch_sem"] = dma((2, 2))
    scratch["push_sem"] = scratch["land_sem"] = dma((2, blocks))
    names = list(scalars) + list(vectors) + list(arrays) + list(outs) + list(scratch)
    smem = pl.BlockSpec(memory_space=pltpu.SMEM)
    results = pl.pallas_call(
        functools.partial(layer_kernel, n_row, n_dp, names),
        out_shape=tuple(shape(s, t) for s, t, _ in outs.values()),
        in_specs=[smem] * len(scalars) + [VMEM] * len(vectors) + [ANY] * len(arrays),
        out_specs=tuple(spec for _, _, spec in outs.values()),
        scratch_shapes=list(scratch.values()),
        compiler_params=pltpu.CompilerParams(
            collective_id=0, has_side_effects=True, vmem_limit_bytes=63 << 20
        ),
    )(*scalars.values(), *vectors.values(), *arrays.values())
    return dict(zip(outs, results))


def per_device(
    tokens, encoder, layer_pick, piece_heads, piece_ffn, tgt_len, src_len, norm_gain, norm_shift,
    out_bias, w_self, o_self, b_self, w_cross, o_cross, b_cross, w_up, b_up, w_down, cotangent,
):
    n_row, n_dp = lax.axis_size("row"), lax.axis_size("dp")
    r, d, c = place()
    width = tokens.shape[1]
    units, hw = w_up.shape[1], w_self.shape[2]
    ublk = 256
    out = layer(
        n_row, n_dp,
        dict(
            layer_pick=layer_pick, piece_heads=piece_heads, piece_ffn=piece_ffn,
            tgt_len=tgt_len, src_len=src_len,
        ),
        dict(
            norm_gain=norm_gain, norm_shift=norm_shift, out_bias=out_bias,
            b_self=b_self, b_cross=b_cross, b_up=b_up.reshape(-1, ublk),
        ),
        dict(
            tokens=tokens, cotangent=cotangent, encoder=encoder.reshape(-1, width),
            w_self=jnp.swapaxes(w_self, 1, 2), o_self=o_self,
            w_cross=jnp.swapaxes(w_cross, 1, 2), o_cross=o_cross, w_up=w_up, w_down=w_down,
        ),
    )
    share = width // n_row // n_dp
    small = out["small"]
    if n_dp == 4:
        _, start_of = window(2 * share, share)
        across = lax.rem(d, 2)
        shards = [
            lax.dynamic_slice_in_dim(
                out["shard_" + name], share * across - start_of(across), share
            )
            for name in "sxud"
        ]
    else:
        shards = [
            lax.psum_scatter(
                out["held_" + name].astype(F32).reshape(width, -1),
                ("row", "dp"), scatter_dimension=0, tiled=True,
            )
            for name in "sxud"
        ]
        small = lax.psum(small, ("row", "dp", "mp"))

    def both(mine, other):
        return jnp.where(
            c == 0, jnp.concatenate([mine, other]), jnp.concatenate([other, mine])
        )

    mine = lax.dynamic_index_in_dim(layer_pick, r, 1, keepdims=False).astype(F32)
    totals = jnp.sum(layer_pick.astype(F32), axis=1)
    grad_encoder = (mine / totals)[:, None, None, None] * out["glad"].astype(F32)
    at = (r * n_dp + d) * share
    norms = lax.dynamic_slice_in_dim(small[:9], at, share, axis=1)
    heads = lax.dynamic_slice_in_dim(small, 16 + 8 * c, 8)[:4, :hw]
    ups = lax.dynamic_slice_in_dim(small, 32 + 8 * c, 8)[: units // ublk, :ublk]
    cut = lambda v, i: v[:, i * hw : (i + 1) * hw]
    w_s, w_x, w_u, w_d = shards
    return (
        both(out["block"], out["block_in"]),
        both(out["gtok"], out["gtok_in"]),
        grad_encoder.reshape(1, -1, width),
        norms[0:3],
        norms[3:6],
        norms[6:9],
        jnp.stack([cut(w_s, 0), cut(w_s, 1), cut(w_s, 2)]),
        cut(w_s, 3).T,
        heads[0:2],
        jnp.stack([cut(w_x, 2), cut(w_x, 0), cut(w_x, 1)]),
        cut(w_x, 3).T,
        heads[2:4],
        w_u,
        ups.reshape(units),
        w_d.T,
    )


def solution(mesh):
    return jax.shard_map(
        per_device,
        mesh=mesh,
        in_specs=(
            P(("row", "dp"), None),
            P("row", "dp", None),
            P(),
            P(),
            P(),
            P(("row", "dp")),
            P(("row", "dp")),
            P(),
            P(),
            P(),
            P(None, None, "mp"),
            P("mp", None),
            P(None, "mp"),
            P(None, None, "mp"),
            P("mp", None),
            P(None, "mp"),
            P(None, "mp"),
            P("mp"),
            P("mp", None),
            P(("row", "dp"), None),
        ),
        out_specs=(
            P(("row", "dp"), None),
            P(("row", "dp"), None),
            P("row", "dp", None),
            P(None, ("row", "dp")),
            P(None, ("row", "dp")),
            P(None, ("row", "dp")),
            P(None, ("row", "dp"), "mp"),
            P("mp", ("row", "dp")),
            P(None, "mp"),
            P(None, ("row", "dp"), "mp"),
            P("mp", ("row", "dp")),
            P(None, "mp"),
            P(("row", "dp"), "mp"),
            P("mp"),
            P("mp", ("row", "dp")),
        ),
        check_vma=False,
    )
```

time: 1390 us -> 232 us (0.17)
  waiting for transfers between devices: 1000 us -> 0 us
  Pallas kernels: 0 us -> 206 us
  matrix products: 130 us -> 0 us
  local copies, waits for them, and re-layouts: 93.3 us -> 7.06 us
  blocking collectives: 75.7 us -> 0 us
  other arithmetic: 45.4 us -> 16.4 us
  between operations: 16.3 us -> 0.71 us
  starting transfers between devices: 14.4 us -> 0 us
    unnamed x13 -> x0, waiting for transfers between devices: 597 us -> none
    reduce_scatter x2 -> x0, waiting for transfers between devices: 279 us -> none  [the longest x1 139 us: per_device(): lax.psum_scatter(grad_w_down, ('row', 'dp'), scatter_dimension=1, tiled=T...]
    pallas_call x0 -> x1, Pallas kernels: none -> 206 us  [layer(): pl.pallas_call(functools.partial(layer_kernel, n_row, n_dp, names), out_s...]
    dot_general x35 -> x0, matrix products: 130 us -> none  [the longest x2 17.5 us: attend_backward(): jnp.einsum('ghqk,gqhd->gkhd', grad_score, query_low, preferred_element_ty...]
    unnamed x1 -> x0, blocking collectives: 75.7 us -> none
    psum x5 -> x0, waiting for transfers between devices: 74.2 us -> none  [the longest x1 23.3 us: per_device(): lax.psum(jnp.dot(attn_one, o_self, preferred_element_type=jnp.float32), '...]
    all_to_all x2 -> x0, waiting for transfers between devices: 51.9 us -> none  [the longest x1 51.9 us: per_device(): lax.all_to_all(stacked, 'row', split_axis=0, concat_axis=0, tiled=True)]
    unnamed x148 -> x10, local copies, waits for them, and re-layouts: 38.7 us -> 0.02 us
  transfers between devices with their start and end apart: 12 -> 0, of which waited for: 11 -> 0; matrix products, arithmetic and copies ran while one was open for 9% -> 0% of each run, Pallas kernels for 0% -> 0%
where the time goes in v2:
time: 232 us; the launch traced here: 230 us
  Pallas kernels  206 us (89%)
  other arithmetic  16.4 us (7%)
  local copies, waits for them, and re-layouts  7.06 us (3%)
    pallas_call x1, Pallas kernels, layer(): pl.pallas_call(functools.partial(layer_kernel, n_row, n_dp, names), out_s...  206 us
    mul x1, other arithmetic, per_device(): (mine / totals)[:, None, None, None] * out['glad'].astype(F32)  7.54 us
    select_n x1, other arithmetic, both(): jnp.where(c == 0, jnp.concatenate([mine, other]), jnp.concatenate([other,...  7.15 us

profile of v2, /device:TPU:0, one launch (start us, length us, event | category | flops | bytes accessed | tf_op | source)
XLA Modules:
  0.0 230.4 jit_solution(13540950618126631659)
XLA Ops:
  0.6 1.3 reshape.51.args_10_
  1.9 206.3 %shard_map.307 = (f32[512,640]{1,0:T(8,128)}, f32[512,640]{1,0:T(8,128)}, f32[512,640]{1,0:T(8,128)}, f32[512,640]{1,0:T(8,128)}, bf16[4,2,512,640]{3,2,1,0:T(8,...) custom-call(s32[4,4]{1,0:T(4,128)} %args_0_.4, ...), custom_call_target="tpu_custom_call" | custom-call | tf_op jit(solution)/shard_map/pallas_call | solution.py:721
  208.2 0.0 copy-start.4
  208.2 7.1 %maximum_select_fusion = (f32[1024,640]{1,0:T(8,128)}, f32[1024,640]{1,0:T(8,128)}) fusion(f32[512,640]{1,0:T(8,128)} %get-tuple-element.26, f32[512,640]{1,0:T(8,128)} %get-tuple-element.25, pred[]{:T(512)S(6)} %eq.4, f32[512,640]{1,0:T(8,128)} %get-tuple-element.27, f32[512,640]{1,0:T(8,128)} %get-tuple-element.28), kind=kLoop, calls=%fused_computation.1 | loop fusion | flops 3932160 | bytes 10485761 | tf_op jit(solution)/shard_map/jit(_where)/select_n | solution.py:781
  215.4 0.0 copy-done.4
  215.4 0.2 fusion.1
  215.6 0.1 convert_reduce_fusion
  215.7 0.0 copy-start
  215.7 0.0 copy-start.1
  215.7 0.0 copy-start.2
  215.7 0.0 copy-start.3
  215.7 7.5 %convert_multiply_fusion = f32[4,2,512,640]{3,2,1,0:T(8,128)} fusion(bf16[4,2,512,640]{3,2,1,0:T(8,128)(2,1)} %get-tuple-element.29, f32[4]{0:T(128)S(1)} %div.18), kind=kLoop, calls=%fused_computation | loop fusion | flops 5242880 | bytes 15728656 | tf_op jit(solution)/shard_map/mul | solution.py:787
  223.3 0.8 slice.48
  224.0 0.7 fusion.2
  224.7 0.0 copy-done
  224.7 0.0 copy-done.1
  224.7 0.8 dynamic-slice_bitcast_fusion.1
  225.5 0.7 pad_maximum_fusion
  226.2 1.4 constant_dynamic-slice_fusion.4
  227.6 0.7 pad_maximum_fusion.1
  228.3 0.0 copy-done.2
  228.3 0.0 copy-done.3
  228.3 0.8 dynamic-slice_bitcast_fusion
  229.1 0.7 constant_dynamic-slice_fusion.2
  229.8 0.6 reshape.54
  (1 shorter events, 0.0 us)
Async XLA Ops:
  208.2 7.2 %copy-start.4 = (s32[4,4]{1,0:T(4,128)S(1)}, s32[4,4]{1,0:T(4,128)}, u32[]{:S(2)}) copy-start(s32[4,4]{1,0:T(4,128)} %args_0_.4) | copy-start | bytes 196
  215.7 9.0 %copy-start = (f32[48,1280]{1,0:T(8,128)S(1)}, f32[48,1280]{1,0:T(8,128)}, u32[]{:S(2)}) copy-start(f32[48,1280]{1,0:T(8,128)} %get-tuple-element.31) | copy-start | bytes 737284
  215.7 9.0 %copy-start.1 = (f32[48,1280]{1,0:T(8,128)S(1)}, f32[48,1280]{1,0:T(8,128)}, u32[]{:S(2)}) copy-start(f32[48,1280]{1,0:T(8,128)} %get-tuple-element.32) | copy-start | bytes 737284
  215.7 12.6 %copy-start.2 = (f32[48,1536]{1,0:T(8,128)S(1)}, f32[48,1536]{1,0:T(8,128)}, u32[]{:S(2)}) copy-start(f32[48,1536]{1,0:T(8,128)} %get-tuple-element.33) | copy-start | bytes 884740
  215.7 12.5 %copy-start.3 = (f32[48,1536]{1,0:T(8,128)S(1)}, f32[48,1536]{1,0:T(8,128)}, u32[]{:S(2)}) copy-start(f32[48,1536]{1,0:T(8,128)} %get-tuple-element.34) | copy-start | bytes 884740
